TPU v7x, 32 devices: a whole 2x2x4 slice. The times are simulated.
32 devices in a mesh: groups: 1, dp: 4 (over y, x), tensor: 8 (over z, core).
Axes of the slice: x: 2, y: 2, z: 4, core: 2. Of those that a mesh axis runs over, the one named last changes fastest.
Arguments:
- tokens: bfloat16 [512, 4096], P(('groups', 'dp', 'tensor')), may hold values from -6 to 6
- grad_out: bfloat16 [512, 4096], P(('groups', 'dp', 'tensor')), may hold values from -1.5 to 1.5
- gate_weight: bfloat16 [4096, 16384], P('dp', 'tensor'), may hold values from -0.09375 to 0.09375
- up_weight: bfloat16 [4096, 16384], P('dp', 'tensor'), may hold values from -0.09375 to 0.09375
- down_weight: bfloat16 [16384, 4096], P('tensor', 'dp'), may hold values from -0.09375 to 0.09375
- block_kind: int32 [160], P('tensor'), may hold values from 0 to 2
- block_ff: int32 [160], P('tensor'), may hold values from 0 to 15
- block_d: int32 [160], P('tensor'), may hold values from 0 to 31
- block_owner: int32 [160, 1], P('tensor'), may hold values from 0 to 3; in each aligned block of 20 rows (0 to 19, 20 to 39, ...) at most 5 rows name the same one
Outputs:
- grad_tokens: bfloat16 [512, 4096], P(('groups', 'dp', 'tensor'))
- delta_grads: float32 [160, 128, 128], P(('groups', 'dp', 'tensor'))
Inputs may be any that keep to these rules, and one draw needn't show every extreme that they name: `block_owner`: among the 20 entries of one index of tensor no owner appears more than 5 times, and some owner appears exactly 5 times.
All inputs are finite; a program needn't handle non-finite values.
Results may differ from a plain program's by a relative error of at most 0.0095.
Values may be sent and summed in bfloat16 or wider, within the bound.
No kernel may reach another device: no remote copies, remote signals or barrier semaphores. Data moves between devices by JAX's collectives and lax.ppermute only.
A program may use at most 192 MiB of HBM per device.

v0:
```python
import functools

import jax
import jax.numpy as jnp
import numpy as np
from jax import lax
from jax.experimental import pallas as pl
from jax.experimental.pallas import tpu as pltpu
from jax.sharding import PartitionSpec as P

BLOCK = 128
CAP = 5
CONTRACT_LAST = (((1,), (1,)), ((), ()))
SMALL = pl.CostEstimate(flops=1, bytes_accessed=1, transcendentals=0)


def xor_perm(size, mask):
    return [(i, i ^ mask) for i in range(size)]


def z_perm(n_tensor, mask):
    return [(rank, rank ^ 2 * mask) for rank in range(n_tensor)]


def chunk_masks(n_z):
    low, high = tuple(range(n_z // 2)), tuple(range(n_z // 2, n_z))
    return {"own": low[:1], "near": low[1:], 0: low, 1: high, "rest": low[1:] + high}


def delta_kernel(n_dp, n_pieces, me_ref, kind_ref, ff_ref, col_ref, owner_ref, *refs):
    window_refs, refs = refs[:2], refs[2:]
    hidden_refs, grad_refs, refs = refs[:n_pieces], refs[n_pieces : 2 * n_pieces], refs[2 * n_pieces :]
    out_ref, grads_ref, tokens_ref, hidden_ref, gate_ref, up_ref, used_ref = refs
    me = me_ref[0]
    out_ref[...] = jnp.zeros_like(out_ref)
    for owner in range(n_dp):
        used_ref[owner] = 0

    start = 0
    _, chips, rows, _ = window_refs[0].shape
    for chip in range(chips):
        for window_ref in window_refs:
            grads_ref[start : start + rows] = window_ref[0, chip]
            tokens_ref[start : start + rows] = window_ref[1, chip]
            start += rows
    start, column = 0, 0
    for hidden_piece, grad_piece in zip(hidden_refs, grad_refs):
        rows, units = hidden_piece.shape
        place = (slice(start, start + rows), slice(column, column + units))
        hidden_ref[place] = hidden_piece[...]
        gate_ref[place] = grad_piece[0]
        up_ref[place] = grad_piece[1]
        column += units
        if column == hidden_ref.shape[1]:
            start, column = start + rows, 0

    def step(entry, carry):
        owner = owner_ref[entry]
        slot = used_ref[owner]
        used_ref[owner] = slot + 1
        kind = kind_ref[entry]
        units = pl.ds(pl.multiple_of(ff_ref[entry] * BLOCK, BLOCK), BLOCK)
        columns = pl.ds(pl.multiple_of(col_ref[entry] * BLOCK, BLOCK), BLOCK)
        left = jnp.where(kind == 2, hidden_ref[:, units], tokens_ref[:, columns])
        right = jnp.where(
            kind == 0,
            gate_ref[:, units],
            jnp.where(kind == 1, up_ref[:, units], grads_ref[:, columns]),
        )
        out_ref[(owner ^ me) * CAP + slot] = lax.dot_general(
            left, right, (((0,), (0,)), ((), ())), preferred_element_type=jnp.float32
        )
        return carry

    lax.fori_loop(0, kind_ref.shape[0], step, 0)


def window_deltas(n_dp, units, me, kind, ff, col, owner, windows, hiddens, grads):
    _, chips, rows, features = windows[0].shape
    total = 2 * chips * rows
    if rows % 16:
        joined = jnp.stack(windows, axis=2).reshape(2, 1, total, features)
        windows = [joined[:, :, : total // 2], joined[:, :, total // 2 :]]
        across = units // hiddens[0].shape[1]
        groups = range(0, len(hiddens), across)
        hiddens = [
            jnp.concatenate([jnp.concatenate(hiddens[i : i + across], axis=1) for i in groups])
        ]
        grads = [
            jnp.concatenate([jnp.concatenate(grads[i : i + across], axis=2) for i in groups], axis=1)
        ]
    smem, vmem = pl.BlockSpec(memory_space=pltpu.SMEM), pl.BlockSpec(memory_space=pltpu.VMEM)
    bf16 = jnp.bfloat16
    return pl.pallas_call(
        functools.partial(delta_kernel, n_dp, len(hiddens)),
        out_shape=jax.ShapeDtypeStruct((n_dp * CAP, BLOCK, BLOCK), jnp.float32),
        in_specs=[smem] * 5 + [vmem] * (2 + 2 * len(hiddens)),
        out_specs=vmem,
        scratch_shapes=[
            pltpu.VMEM((total, features), bf16),
            pltpu.VMEM((total, features), bf16),
            pltpu.VMEM((total, units), bf16),
            pltpu.VMEM((total, units), bf16),
            pltpu.VMEM((total, units), bf16),
            pltpu.SMEM((n_dp,), jnp.int32),
        ],
        compiler_params=pltpu.CompilerParams(vmem_limit_bytes=24 << 20),
        cost_estimate=SMALL,
    )(me.reshape(1), kind, ff, col, owner, *windows, *hiddens, *grads)


def load_kernel(*refs):
    n = (len(refs) - 1) // 2
    copies = [
        pltpu.make_async_copy(source, target, refs[-1].at[i])
        for i, (source, target) in enumerate(zip(refs[:n], refs[n : 2 * n]))
    ]
    for copy in copies:
        copy.start()
    for copy in copies:
        copy.wait()


def in_vmem(*weights):
    return pl.pallas_call(
        load_kernel,
        out_shape=[pltpu.VMEM(w.shape, w.dtype) for w in weights],
        in_specs=[pl.BlockSpec(memory_space=pl.ANY)] * len(weights),
        out_specs=[pl.BlockSpec(memory_space=pltpu.VMEM)] * len(weights),
        scratch_shapes=[pltpu.SemaphoreType.DMA((len(weights),))],
        compiler_params=pltpu.CompilerParams(vmem_limit_bytes=1 << 20),
        cost_estimate=SMALL,
    )(*[pltpu.with_memory_space_constraint(w, pltpu.HBM) for w in weights])


def forward_kernel(bits, own_ref, other_ref, gate_ref, up_ref, down_ref, *refs):
    out_refs, chunk_ref = refs[:-1], refs[-1]
    f32 = jnp.float32
    chips, _, windows, rows, _ = own_ref.shape
    start = 0
    for window in range(windows):
        for chip in range(chips):
            for ref in (own_ref, other_ref):
                chunk_ref[:, start : start + rows] = ref[chip, :, window]
                start += rows
    count = start // windows
    grads, tokens = chunk_ref[0], chunk_ref[1]
    part = out_refs[0].shape[3]
    block = min(part, 512)
    for q, bit in enumerate(bits):
        for column in range(0, part, block):
            units = slice(q * part + column, q * part + column + block)
            products = (
                jnp.dot(tokens, gate_ref[:, units], preferred_element_type=f32),
                jnp.dot(tokens, up_ref[:, units], preferred_element_type=f32),
                lax.dot_general(
                    grads, down_ref[units, :], CONTRACT_LAST, preferred_element_type=f32
                ),
            )
            for i, product in enumerate(products):
                product = product.astype(chunk_ref.dtype)
                places = [0, 0]
                for window in range(windows):
                    sent = window >> bit & 1
                    out_refs[2 * q + sent][i, places[sent], :, column : column + block] = product[
                        window * count : (window + 1) * count
                    ]
                    places[sent] += 1


def forward_partials(bits, own, other, gate_weight, up_weight, down_weight):
    chips, _, windows, rows, width = own.shape
    count = 2 * chips * rows
    part = gate_weight.shape[1] // len(bits)
    vmem = pl.BlockSpec(memory_space=pltpu.VMEM)
    outs = pl.pallas_call(
        functools.partial(forward_kernel, bits),
        out_shape=[jax.ShapeDtypeStruct((3, windows // 2, count, part), own.dtype)] * 2 * len(bits),
        in_specs=[vmem] * 5,
        out_specs=[vmem] * 2 * len(bits),
        scratch_shapes=[pltpu.VMEM((2, windows * count, width), own.dtype)],
        compiler_params=pltpu.CompilerParams(vmem_limit_bytes=16 << 20),
        cost_estimate=SMALL if chips > 1 else pl.CostEstimate(
            flops=1*6 * windows * count * width * gate_weight.shape[1],
            bytes_accessed=3 * width * gate_weight.shape[1],
            transcendentals=0,
        ),
    )(own, other, gate_weight, up_weight, down_weight)
    return outs[::2], outs[1::2]


def backward_kernel(places, *refs):
    f32 = jnp.float32
    n = len(places)
    piece_refs, (gate_ref, up_ref, out_ref, grads_ref) = refs[:n], refs[n:]
    for piece_ref, (starts, column) in zip(piece_refs, places):
        _, _, rows, columns = piece_ref.shape
        for index, start in enumerate(starts):
            place = (slice(None), slice(start, start + rows), slice(column, column + columns))
            grads_ref[place] = piece_ref[index]
    width = out_ref.shape[1]
    block = min(width, 256)
    for column in range(0, width, block):
        cut = slice(column, column + block)
        first = lax.dot_general(
            grads_ref[0], gate_ref[cut, :], CONTRACT_LAST, preferred_element_type=f32
        )
        second = lax.dot_general(
            grads_ref[1], up_ref[cut, :], CONTRACT_LAST, preferred_element_type=f32
        )
        out_ref[:, cut] = first + second


def backward_partials(pieces, places, gate_weight, up_weight):
    width, units = gate_weight.shape
    total = max(start for starts, _ in places for start in starts) + pieces[0].shape[2]
    vmem = pl.BlockSpec(memory_space=pltpu.VMEM)
    return pl.pallas_call(
        functools.partial(backward_kernel, places),
        out_shape=jax.ShapeDtypeStruct((total, width), jnp.float32),
        in_specs=[vmem] * (len(pieces) + 2),
        out_specs=vmem,
        scratch_shapes=[pltpu.VMEM((2, total, units), jnp.bfloat16)],
        compiler_params=pltpu.CompilerParams(vmem_limit_bytes=16 << 20),
        cost_estimate=SMALL,
    )(*pieces, gate_weight, up_weight)


def place_kernel(me_ref, *refs):
    piece_refs, out_ref = refs[:-1], refs[-1]
    width = piece_refs[0].shape[1]
    for mask, piece_ref in enumerate(piece_refs):
        start = pl.multiple_of((me_ref[0] ^ mask) * width, BLOCK)
        out_ref[:, pl.ds(start, width)] = piece_ref[...]


def place_slices(me, pieces):
    smem, vmem = pl.BlockSpec(memory_space=pltpu.SMEM), pl.BlockSpec(memory_space=pltpu.VMEM)
    rows, width = pieces[0].shape
    return pl.pallas_call(
        place_kernel,
        out_shape=jax.ShapeDtypeStruct((rows, width * len(pieces)), pieces[0].dtype),
        in_specs=[smem] + [vmem] * len(pieces),
        out_specs=vmem,
        compiler_params=pltpu.CompilerParams(vmem_limit_bytes=4 << 20),
        cost_estimate=SMALL,
    )(me.reshape(1), *pieces)


def body(
    tokens,
    grad_out,
    gate_weight,
    up_weight,
    down_weight,
    block_kind,
    block_ff,
    block_d,
    block_owner,
):
    n_dp, n_tensor = lax.axis_size("dp"), lax.axis_size("tensor")
    n_z = n_tensor // 2
    bits = n_dp.bit_length() - 1
    rows, features = tokens.shape
    width, units = gate_weight.shape
    me = lax.axis_index("dp")
    bf16, f32 = jnp.bfloat16, jnp.float32
    parts = min(bits, 2)
    part = units // parts
    orders = [[(q + s) % bits for s in range(bits)] for q in range(parts)]
    masks = chunk_masks(n_z)
    stages = 2 * bits

    chain = []

    def ordered(*values):
        if not chain:
            return values
        return lax.optimization_barrier(values + tuple(chain))[: len(values)]

    def done(*results):
        chain[:] = results

    def over_dp(value, mask):
        return lax.ppermute(value, "dp", xor_perm(n_dp, mask))

    def over_core(value):
        return lax.ppermute(value, "tensor", xor_perm(n_tensor, 1))

    def over_z(value, mask):
        return lax.ppermute(value, "tensor", z_perm(n_tensor, mask))

    held, window_held, shards, other = {}, {}, {}, {}
    ready, flying, local, owns, out_flying, terms = {}, {}, {}, {}, {}, {}

    def hop(held, mask):
        low = mask & -mask
        held[mask] = over_z(held[mask ^ low], low)

    def relay(held, mask):
        (held[mask],) = ordered(held[mask])
        low = mask & -mask if mask else n_z
        for step in range(low.bit_length() - 1):
            hop(held, mask | 1 << step)

    def swap(k):
        got = ordered(*[held[mask] for mask in masks[k]])
        shards[k] = jnp.stack(got)
        other[k] = over_core(shards[k])
        done(shards[k])

    pieces = []
    for mask in range(n_dp):
        start = (me ^ mask) * width
        piece = jnp.stack(
            [lax.dynamic_slice_in_dim(x, start, width, axis=1) for x in (grad_out, tokens)]
        )
        pieces.append(over_dp(piece, mask) if mask else piece)
    if rows % 16 == 0:
        gate_weight, up_weight, down_weight = in_vmem(gate_weight, up_weight, down_weight)
        done(gate_weight, up_weight, down_weight)
    held[0] = jnp.stack(ordered(*pieces), axis=1)
    for step in range(n_z.bit_length() - 1):
        hop(held, 1 << step)

    def forward(k):
        own, others = ordered(shards[k], other[k])
        weights = (gate_weight, up_weight, down_weight)
        if rows % 16 == 0:
            first = [order[0] for order in orders]
            keep, fly = forward_partials(first, own, others, *weights)
            shape = (3,) + (2,) * (bits - 1) + (-1, part)
            local[k] = [x.reshape(shape) for x in keep]
            ready[k] = [x.reshape(shape) for x in fly]
            done(*local[k], *ready[k])
            return
        chunk = jnp.stack([own, others], axis=3).transpose(1, 2, 0, 3, 4, 5)
        chunk = chunk.reshape(2, -1, width)
        gate = jnp.dot(chunk[1], gate_weight, preferred_element_type=f32).astype(bf16)
        upward = jnp.dot(chunk[1], up_weight, preferred_element_type=f32).astype(bf16)
        hidden_grad = lax.dot_general(
            chunk[0], down_weight, CONTRACT_LAST, preferred_element_type=f32
        ).astype(bf16)
        sums = jnp.stack([gate, upward, hidden_grad])
        values = []
        for q in range(parts):
            value = sums[:, :, q * part : (q + 1) * part]
            values.append(value.reshape((3,) + (2,) * bits + (-1, part)))
        ready[k] = values
        done(*values)

    def add_halves(keep, fly):
        got = ordered(*fly)
        return [x.astype(f32) + y.astype(f32) for x, y in zip(keep, got)]

    def gradients(sums):
        hiddens, values = [], []
        for g, u, h in sums:
            sig = jax.nn.sigmoid(g)
            silu = g * sig
            hiddens.append((silu * u).astype(bf16))
            gate_grad = (h * u * sig * (1.0 + g * (1.0 - sig))).astype(bf16)
            up_grad = (h * silu).astype(bf16)
            values.append(jnp.stack([gate_grad, up_grad]))
        return hiddens, values

    def join(values, got, s):
        joined = []
        for value, more, order in zip(values, got, orders):
            order = order[::-1]
            axis = sum(1 for bit in order[:s] if bit > order[s])
            joined.append(jnp.stack([value, more], axis=axis))
        return joined

    def send(k, s):
        values = ordered(*ready[k])
        if s >= bits:
            local[k] = values
            flying[k] = [
                over_dp(value, 1 << order[::-1][s - bits]) for value, order in zip(values, orders)
            ]
            return
        if k != "delta" and s == 0 and rows % 16 == 0:
            flying[k] = [over_dp(x, 1 << order[s]) for x, order in zip(values, orders)]
            return
        local[k], fly = [], []
        for value, order in zip(values, orders):
            axis = (k != "delta") + sorted(order[s:], reverse=True).index(order[s])
            local[k].append(lax.index_in_dim(value, 0, axis, keepdims=False))
            fly.append(lax.index_in_dim(value, 1, axis, keepdims=False).astype(bf16))
        flying[k] = [over_dp(x, 1 << order[s]) for x, order in zip(fly, orders)]

    def take(k, s):
        if s < bits:
            values = add_halves(local[k], flying[k])
            if k == "delta":
                ready[k] = values
                done(*values)
                return
        else:
            values = join(local[k], ordered(*flying[k]), s - bits)
        if s == bits - 1:
            hiddens, values = gradients(values)
            owns[k] = (hiddens, values)
            done(*hiddens, *values)
        else:
            done(*values)
        ready[k] = values

    def merge():
        ready[0] = [
            jnp.concatenate(values, axis=-2) for values in zip(ready["own"], ready["near"])
        ]
        done(*ready[0])

    def part_again():
        count = 2 * rows
        ready["own"] = [x[..., :count, :] for x in ready[0]]
        ready["rest"] = [
            jnp.concatenate([x[..., count:, :], y], axis=-2) for x, y in zip(ready[0], ready[1])
        ]
        done(*ready["rest"])

    def finish(k):
        got = ordered(*flying[k])
        if rows % 16 == 0:
            count = 2 * len(masks[k]) * rows
            pieces, places = [], []
            for q in range(parts):
                order = orders[q][::-1]
                known = sorted(order[:-1], reverse=True)
                windows = [
                    sum(bit << at for bit, at in zip(index, known))
                    for index in np.ndindex((2,) * (bits - 1))
                ]
                for here, piece in enumerate((local[k][q], got[q])):
                    pieces.append(piece.reshape(-1, 2, count, part))
                    starts = [(window | here << order[-1]) * count for window in windows]
                    places.append((tuple(starts), q * part))
            out = backward_partials(pieces, tuple(places), gate_weight, up_weight)
        else:
            gathered = []
            for value in join(local[k], got, bits - 1):
                value = value.reshape((n_dp, 2, -1, part))
                gathered.append(jnp.swapaxes(value, 0, 1).reshape(2, -1, part))
            gathered = jnp.concatenate(gathered, axis=2)
            out = sum(
                lax.dot_general(x, w, CONTRACT_LAST, preferred_element_type=f32)
                for x, w in zip(gathered, (gate_weight, up_weight))
            )
        out = out.reshape(n_dp, len(masks[k]), 2, rows, width)
        send = out[:, :, 1].astype(bf16)
        out_flying[k] = (out[:, :, 0], over_core(send))
        done(send)

    def send_home(k):
        own, got = out_flying[k]
        (got,) = ordered(got)
        out = own + got.astype(f32)
        for place, mask in enumerate(masks[k]):
            term = out[:, place]
            if mask:
                term = term.astype(bf16)
                terms[mask] = over_z(term, mask)
            else:
                terms[mask] = term
            done(term)

    def collect(sources):
        total = 0.0
        for term in ordered(*[terms[mask] for mask in sources]):
            total = total + term.astype(f32)
        done(total)
        return total

    def window_rows(mask):
        if mask == 0:
            window_held[0] = jnp.stack(ordered(grad_out, tokens))
        else:
            places = list(window_held)
            values = ordered(*[window_held[place] for place in places])
            window_held.update(zip(places, values))
        if mask + 1 < n_z:
            hop(window_held, mask + 1)
            return
        rows_there = [window_held[mask] for k in range(2) for mask in masks[k]]
        window_held["own"] = jnp.stack(rows_there, axis=1)
        window_held["other"] = over_core(window_held["own"])
        done(window_held["own"])

    def delta_terms():
        windows = ordered(window_held["own"], window_held["other"])
        chunks = range(2)
        deltas = window_deltas(
            n_dp,
            units,
            me,
            block_kind,
            block_ff,
            block_d,
            block_owner[:, 0],
            list(windows),
            [piece for k in chunks for piece in owns[k][0]],
            [piece for k in chunks for piece in owns[k][1]],
        )
        done(deltas)
        deltas = deltas.reshape((2,) * bits + (CAP, BLOCK, BLOCK))
        cut = BLOCK // parts
        ready["delta"] = [deltas[..., q * cut : (q + 1) * cut, :] for q in range(parts)]

    swap("own")
    forward("own")
    send("own", 0)
    for mask in masks["near"][1::2]:
        relay(held, mask)
    swap("near")
    for mask in masks[1][::2]:
        relay(held, mask)
    forward("near")
    send("near", 0)
    take("own", 0)
    swap(1)
    take("near", 0)
    merge()
    send(0, 1)
    forward(1)
    send(1, 0)
    window_rows(0)
    hops = iter(range(1, n_z))
    for s in range(2, stages - 1):
        take(0, s - 1)
        send(0, s)
        window_rows(next(hops))
        take(1, s - 2)
        send(1, s - 1)
    for mask in hops:
        window_rows(mask)
    take(1, stages - 3)
    take(0, stages - 2)
    send(1, stages - 2)
    delta_terms()
    send("delta", 0)
    take(1, stages - 2)
    part_again()
    send("rest", stages - 1)
    take("delta", 0)
    send("own", stages - 1)
    finish("rest")
    send_home("rest")
    total = collect(masks["rest"][:1])
    *flying["own"], total = lax.optimization_barrier((*flying["own"], total))
    finish("own")
    for s in range(1, bits):
        if s > 1:
            take("delta", s - 1)
        send("delta", s)
    send_home("own")

    total = total + terms[0] + collect(masks["rest"][1:])
    total = total.astype(bf16)
    pieces = [total[0]] + [over_dp(total[mask], mask) for mask in range(1, n_dp)]
    done(total)
    take("delta", bits - 1)
    deltas = jnp.concatenate(ready["delta"], axis=1)
    grad_tokens = place_slices(me, pieces)
    return (grad_tokens, deltas)


def solution(mesh):
    placed = (
        P(("groups", "dp", "tensor"), None),
        P(("groups", "dp", "tensor"), None),
        P("dp", "tensor"),
        P("dp", "tensor"),
        P("tensor", "dp"),
        P("tensor"),
        P("tensor"),
        P("tensor"),
        P("tensor", None),
    )
    return jax.shard_map(
        body,
        mesh=mesh,
        in_specs=placed,
        out_specs=(P(("groups", "dp", "tensor"), None), P(("groups", "dp", "tensor"), None, None)),
        check_vma=False,
    )
```

profile of v0, /device:TPU:0, one launch (start us, length us, event | category | flops | bytes accessed | tf_op | source)
XLA Modules:
  0.0 146.4 jit_solution(8612901397078912225)
XLA Ops:
  1.6 3.0 %collective-permute-start = (bf16[2,16,1024]{2,1,0:T(8,128)(2,1)S(1)}, bf16[2,16,1024]{2,1,0:T(8,128)(2,1)S(1)}, u32[]{:S(2)}, u32[]{:S(2)}) collective-permute-start(bf16[2,16,1024]{2,1,0:T(8,128)(2,1)S(1)} %pad_maximum_fusion.14), channel_id=1, source_target_pairs={{0,8},{8,0},{16,24},{24,16},{1,9},{9,1},{17,25},{25,17},{2,10},{10... | collective-permute-start | bytes 196616 | tf_op jit(solution)/shard_map/ppermute | solution.py:285
  6.2 4.7 %shard_map.104 = (bf16[1024,2048]{1,0:T(8,128)(2,1)S(1)}, bf16[1024,2048]{1,0:T(8,128)(2,1)S(1)}, bf16[2048,1024]{1,0:T(8,128)(2,1)S(1)}) custom-call(bf16[1024,2048]{1,0:T(8,128)(2,1)} %refs_0_.1, bf16[1024,2048]{1,0:T(8,128)(2,1)} %refs_1_.1, bf16[2048,1024]{1,0:T(8,128)(2,1)} %refs_2_.1), custom_call_target="tpu_custom_call" | custom-call | flops 1 | bytes 1 | tf_op jit(solution)/shard_map/pallas_call | solution.py:125
  11.5 1.7 %collective-permute-start.6 = (bf16[2,4,16,1024]{3,2,1,0:T(8,128)(2,1)S(1)}, bf16[2,4,16,1024]{3,2,1,0:T(8,128)(2,1)S(1)}, u32[]{:S(2)}, u32[]{:S(2)}) collective-permute-start(bf16[2,4,16,1024]{3,2,1,0:T(8,128)(2,1)S(1)} %pad_maximum_fusion.7), channel_id=1, source_target_pairs={{0,2},{1,3},{2,0},{3,1},{4,6},{5,7},{6,4},{7,5},{8,10},{9,11},{10,... | collective-permute-start | bytes 786440 | tf_op jit(solution)/shard_map/ppermute | solution.py:291
  13.2 2.6 %collective-permute-start.10 = (bf16[2,4,16,1024]{3,2,1,0:T(8,128)(2,1)S(1)}, bf16[2,4,16,1024]{3,2,1,0:T(8,128)(2,1)S(1)}, u32[]{:S(2)}, u32[]{:S(2)}) collective-permute-start(bf16[2,4,16,1024]{3,2,1,0:T(8,128)(2,1)S(1)} %pad_maximum_fusion.7), channel_id=1, source_target_pairs={{0,4},{1,5},{2,6},{3,7},{4,0},{5,1},{6,2},{7,3},{8,12},{9,13},{10,... | collective-permute-start | bytes 786440 | tf_op jit(solution)/shard_map/ppermute | solution.py:291
  15.8 2.7 %shard_map.105 = (bf16[3,2,32,1024]{3,2,1,0:T(8,128)(2,1)S(1)}, bf16[3,2,32,1024]{3,2,1,0:T(8,128)(2,1)S(1)}, bf16[3,2,32,1024]{3,2,1,0:T(8,128)(2,1)S(1)}, bf16[3,2,32,1024]{3,2,1,0:T(8,128)(2,1)S(1)}) custom-call(bf16[1,2,4,16,1024]{4,3,2,1,0:T(8,128)(2,1)S(1)} %bitcast.193, bf16[1,2,4,16,1024]{4,3,2,1,0:T(8,128)(2,1)S(1)} %collective-permute-done.3.other_ref, ...), custom_call_target="tpu_custom_call" | custom-call | flops 1610612736 | bytes 6291456 | tf_op jit(solution)/shard_map/pallas_call | solution.py:176
  18.5 7.3 %collective-permute-done.6 = bf16[2,4,16,1024]{3,2,1,0:T(8,128)(2,1)S(1)} collective-permute-done((bf16[2,4,16,1024]{3,2,1,0:T(8,128)(2,1)S(1)}, bf16[2,4,16,1024]{3,2,1,0:T(8,128)(2,1)S(1)}, u32[]{:S(2)}, u32[]{:S(2)}) %collective-permute-start.6) | collective-permute-done | bytes 262176 | tf_op jit(solution)/shard_map/ppermute | solution.py:291
  25.8 1.6 %collective-permute-start.4 = (bf16[3,2,32,1024]{3,2,0,1:T(8,128)(2,1)S(1)}, bf16[3,2,32,1024]{3,2,0,1:T(8,128)(2,1)S(1)}, u32[]{:S(2)}, u32[]{:S(2)}) collective-permute-start(bf16[3,2,32,1024]{3,2,0,1:T(8,128)(2,1)S(1)} %copy.28), channel_id=1, source_target_pairs={{0,8},{8,0},{16,24},{24,16},{1,9},{9,1},{17,25},{25,17},{2,10},{10... | collective-permute-start | bytes 1179656 | tf_op jit(solution)/shard_map/ppermute | solution.py:285
  27.4 1.6 %collective-permute-start.5 = (bf16[3,2,32,1024]{3,2,0,1:T(8,128)(2,1)S(1)}, bf16[3,2,32,1024]{3,2,0,1:T(8,128)(2,1)S(1)}, u32[]{:S(2)}, u32[]{:S(2)}) collective-permute-start(bf16[3,2,32,1024]{3,2,0,1:T(8,128)(2,1)S(1)} %copy.29), channel_id=1, source_target_pairs={{0,16},{8,24},{16,0},{24,8},{1,17},{9,25},{17,1},{25,9},{2,18},{10... | collective-permute-start | bytes 1179656 | tf_op jit(solution)/shard_map/ppermute | solution.py:285
  29.0 2.7 %shard_map.106 = (bf16[3,2,32,1024]{3,2,1,0:T(8,128)(2,1)S(1)}, bf16[3,2,32,1024]{3,2,1,0:T(8,128)(2,1)S(1)}, bf16[3,2,32,1024]{3,2,1,0:T(8,128)(2,1)S(1)}, bf16[3,2,32,1024]{3,2,1,0:T(8,128)(2,1)S(1)}) custom-call(bf16[1,2,4,16,1024]{4,3,2,1,0:T(8,128)(2,1)S(1)} %bitcast.195, bf16[1,2,4,16,1024]{4,3,2,1,0:T(8,128)(2,1)S(1)} %collective-permute-done.7.other_ref, ...), custom_call_target="tpu_custom_call" | custom-call | flops 1610612736 | bytes 6291456 | tf_op jit(solution)/shard_map/pallas_call | solution.py:176
  34.5 3.3 %collective-permute-done.4 = bf16[3,2,32,1024]{3,2,0,1:T(8,128)(2,1)S(1)} collective-permute-done((bf16[3,2,32,1024]{3,2,0,1:T(8,128)(2,1)S(1)}, bf16[3,2,32,1024]{3,2,0,1:T(8,128)(2,1)S(1)}, u32[]{:S(2)}, u32[]{:S(2)}) %collective-permute-start.4) | collective-permute-done | bytes 393248 | tf_op jit(solution)/shard_map/ppermute | solution.py:285
  37.8 1.7 %collective-permute-done.5 = bf16[3,2,32,1024]{3,2,0,1:T(8,128)(2,1)S(1)} collective-permute-done((bf16[3,2,32,1024]{3,2,0,1:T(8,128)(2,1)S(1)}, bf16[3,2,32,1024]{3,2,0,1:T(8,128)(2,1)S(1)}, u32[]{:S(2)}, u32[]{:S(2)}) %collective-permute-start.5) | collective-permute-done | bytes 393248 | tf_op jit(solution)/shard_map/ppermute | solution.py:285
  39.8 6.0 %collective-permute-done.8 = bf16[3,2,32,1024]{3,2,0,1:T(8,128)(2,1)S(1)} collective-permute-done((bf16[3,2,32,1024]{3,2,0,1:T(8,128)(2,1)S(1)}, bf16[3,2,32,1024]{3,2,0,1:T(8,128)(2,1)S(1)}, u32[]{:S(2)}, u32[]{:S(2)}) %collective-permute-start.8) | collective-permute-done | bytes 393248 | tf_op jit(solution)/shard_map/ppermute | solution.py:285
  50.1 3.5 %shard_map.107 = (bf16[3,2,64,1024]{3,2,1,0:T(8,128)(2,1)S(1)}, bf16[3,2,64,1024]{3,2,1,0:T(8,128)(2,1)S(1)}, bf16[3,2,64,1024]{3,2,1,0:T(8,128)(2,1)S(1)}, bf16[3,2,64,1024]{3,2,1,0:T(8,128)(2,1)S(1)}) custom-call(bf16[2,2,4,16,1024]{4,3,2,1,0:T(8,128)(2,1)S(1)} %pad_maximum_fusion.5.own_ref, ...), custom_call_target="tpu_custom_call" | custom-call | flops 1 | bytes 1 | tf_op jit(solution)/shard_map/pallas_call | solution.py:176
  55.9 4.0 %collective-permute-done.12 = bf16[3,64,1024]{2,1,0:T(8,128)(2,1)S(1)} collective-permute-done((bf16[3,64,1024]{2,1,0:T(8,128)(2,1)S(1)}, bf16[3,64,1024]{2,1,0:T(8,128)(2,1)S(1)}, u32[]{:S(2)}, u32[]{:S(2)}) %collective-permute-start.12) | collective-permute-done | bytes 393248 | tf_op jit(solution)/shard_map/ppermute | solution.py:285
  59.9 1.6 %collective-permute-done.13 = bf16[3,64,1024]{2,1,0:T(8,128)(2,1)S(1)} collective-permute-done((bf16[3,64,1024]{2,1,0:T(8,128)(2,1)S(1)}, bf16[3,64,1024]{2,1,0:T(8,128)(2,1)S(1)}, u32[]{:S(2)}, u32[]{:S(2)}) %collective-permute-start.13) | collective-permute-done | bytes 393248 | tf_op jit(solution)/shard_map/ppermute | solution.py:285
  64.0 14.4 %collective-permute-done.17 = bf16[3,2,64,1024]{3,2,0,1:T(8,128)(2,1)S(1)} collective-permute-done((bf16[3,2,64,1024]{3,2,0,1:T(8,128)(2,1)S(1)}, bf16[3,2,64,1024]{3,2,0,1:T(8,128)(2,1)S(1)}, u32[]{:S(2)}, u32[]{:S(2)}) %collective-permute-start.17) | collective-permute-done | bytes 786464 | tf_op jit(solution)/shard_map/ppermute | solution.py:285
  80.3 5.1 %collective-permute-done.23 = bf16[2,16,4096]{2,1,0:T(8,128)(2,1)S(1)} collective-permute-done((bf16[2,16,4096]{2,1,0:T(8,128)(2,1)S(1)}, bf16[2,16,4096]{2,1,0:T(8,128)(2,1)S(1)}, u32[]{:S(2)}, u32[]{:S(2)}) %collective-permute-start.23) | collective-permute-done | bytes 262176 | tf_op jit(solution)/shard_map/ppermute | solution.py:291
  85.7 3.5 %collective-permute-done.19 = bf16[3,64,1024]{2,1,0:T(8,128)(2,1)S(1)} collective-permute-done((bf16[3,64,1024]{2,1,0:T(8,128)(2,1)S(1)}, bf16[3,64,1024]{2,1,0:T(8,128)(2,1)S(1)}, u32[]{:S(2)}, u32[]{:S(2)}) %collective-permute-start.19) | collective-permute-done | bytes 393248 | tf_op jit(solution)/shard_map/ppermute | solution.py:285
  92.6 5.1 %shard_map.108 = f32[20,128,128]{2,1,0:T(8,128)S(1)} custom-call(s32[1]{0:T(128)} %bitcast.me_ref, s32[20]{0:T(128)S(1)} %copy-done, s32[20]{0:T(128)S(1)} %copy-done.1, s32[20]{0:T(128)S(1)} %copy-done.2, s32[20]{0:T(128)S(1)} %bitcast.196, bf16[2,4,16,4096]{3,2,1,0:T(8,128)(2,1)S(1)} %pad_maximum_fusion.2.refs_0_, ...), custom_call_target="tpu_custom_call" | custom-call | flops 1 | bytes 1 | tf_op jit(solution)/shard_map/pallas_call | solution.py:94
  103.0 15.7 %collective-permute-done.25 = bf16[2,5,64,128]{3,2,1,0:T(8,128)(2,1)S(1)} collective-permute-done((bf16[2,5,64,128]{3,2,1,0:T(8,128)(2,1)S(1)}, bf16[2,5,64,128]{3,2,1,0:T(8,128)(2,1)S(1)}, u32[]{:S(2)}, u32[]{:S(2)}) %collective-permute-start.25) | collective-permute-done | bytes 163872 | tf_op jit(solution)/shard_map/ppermute | solution.py:285
  119.8 3.5 %shard_map.109 = f32[384,1024]{1,0:T(8,128)S(1)} custom-call(bf16[2,2,96,1024]{3,2,1,0:T(8,128)(2,1)S(1)} %maximum_maximum_fusion.refs_0_, bf16[2,2,96,1024]{3,2,1,0:T(8,128)(2,1)S(1)} %collective-permute-done.31.refs_1_, bf16[2,2,96,1024]{3,2,1,0:T(8,128)(2,1)S(1)} %maximum_maximum_fusion.1.refs_2_, ...), custom_call_target="tpu_custom_call" | custom-call | flops 1 | bytes 1 | tf_op jit(solution)/shard_map/pallas_call | solution.py:218
  125.9 3.0 %collective-permute-start.36 = (bf16[4,16,1024]{2,1,0:T(8,128)(2,1)S(1)}, bf16[4,16,1024]{2,1,0:T(8,128)(2,1)S(1)}, u32[]{:S(2)}, u32[]{:S(2)}) collective-permute-start(bf16[4,16,1024]{2,1,0:T(8,128)(2,1)S(1)} %get-tuple-element.207), channel_id=1, source_target_pairs={{0,4},{1,5},{2,6},{3,7},{4,0},{5,1},{6,2},{7,3},{8,12},{9,13},{10,... | collective-permute-start | bytes 393224 | tf_op jit(solution)/shard_map/ppermute | solution.py:291
  130.2 3.1 %collective-permute-done.34 = bf16[4,16,1024]{2,1,0:T(8,128)(2,1)S(1)} collective-permute-done((bf16[4,16,1024]{2,1,0:T(8,128)(2,1)S(1)}, bf16[4,16,1024]{2,1,0:T(8,128)(2,1)S(1)}, u32[]{:S(2)}, u32[]{:S(2)}) %collective-permute-start.34) | collective-permute-done | bytes 131104 | tf_op jit(solution)/shard_map/ppermute | solution.py:291
  133.4 2.9 %shard_map.110 = f32[128,1024]{1,0:T(8,128)S(1)} custom-call(bf16[2,2,32,1024]{3,2,1,0:T(8,128)(2,1)S(1)} %get-tuple-element.172.refs_0_, bf16[2,2,32,1024]{3,2,1,0:T(8,128)(2,1)S(1)} %collective-permute-done.29.refs_1_, bf16[2,2,32,1024]{3,2,1,0:T(8,128)(2,1)S(1)} %get-tuple-element.173.refs_2_, ...), custom_call_target="tpu_custom_call" | custom-call | flops 1 | bytes 1 | tf_op jit(solution)/shard_map/pallas_call | solution.py:218
  (147 shorter events, 40.8 us)
Async XLA Ops:
  11.5 14.2 %collective-permute-start.6 = (bf16[2,4,16,1024]{3,2,1,0:T(8,128)(2,1)S(1)}, bf16[2,4,16,1024]{3,2,1,0:T(8,128)(2,1)S(1)}, u32[]{:S(2)}, u32[]{:S(2)}) collective-permute-start(bf16[2,4,16,1024]{3,2,1,0:T(8,128)(2,1)S(1)} %pad_maximum_fusion.7), channel_id=1, source_target_pairs={{0,2},{1,3},{2,0},{3,1},{4,6},{5,7},{6,4},{7,5},{8,10},{9,11},{10,... | collective-permute-start | bytes 786440 | tf_op jit(solution)/shard_map/ppermute | solution.py:291
  13.2 15.8 %collective-permute-start.10 = (bf16[2,4,16,1024]{3,2,1,0:T(8,128)(2,1)S(1)}, bf16[2,4,16,1024]{3,2,1,0:T(8,128)(2,1)S(1)}, u32[]{:S(2)}, u32[]{:S(2)}) collective-permute-start(bf16[2,4,16,1024]{3,2,1,0:T(8,128)(2,1)S(1)} %pad_maximum_fusion.7), channel_id=1, source_target_pairs={{0,4},{1,5},{2,6},{3,7},{4,0},{5,1},{6,2},{7,3},{8,12},{9,13},{10,... | collective-permute-start | bytes 786440 | tf_op jit(solution)/shard_map/ppermute | solution.py:291
  25.8 12.0 %collective-permute-start.4 = (bf16[3,2,32,1024]{3,2,0,1:T(8,128)(2,1)S(1)}, bf16[3,2,32,1024]{3,2,0,1:T(8,128)(2,1)S(1)}, u32[]{:S(2)}, u32[]{:S(2)}) collective-permute-start(bf16[3,2,32,1024]{3,2,0,1:T(8,128)(2,1)S(1)} %copy.28), channel_id=1, source_target_pairs={{0,8},{8,0},{16,24},{24,16},{1,9},{9,1},{17,25},{25,17},{2,10},{10... | collective-permute-start | bytes 1179656 | tf_op jit(solution)/shard_map/ppermute | solution.py:285
  27.4 12.0 %collective-permute-start.5 = (bf16[3,2,32,1024]{3,2,0,1:T(8,128)(2,1)S(1)}, bf16[3,2,32,1024]{3,2,0,1:T(8,128)(2,1)S(1)}, u32[]{:S(2)}, u32[]{:S(2)}) collective-permute-start(bf16[3,2,32,1024]{3,2,0,1:T(8,128)(2,1)S(1)} %copy.29), channel_id=1, source_target_pairs={{0,16},{8,24},{16,0},{24,8},{1,17},{9,25},{17,1},{25,9},{2,18},{10... | collective-permute-start | bytes 1179656 | tf_op jit(solution)/shard_map/ppermute | solution.py:285
  29.0 10.7 %collective-permute-start.11 = (bf16[2,4,16,1024]{3,2,1,0:T(8,128)(2,1)S(1)}, bf16[2,4,16,1024]{3,2,1,0:T(8,128)(2,1)S(1)}, u32[]{:S(2)}, u32[]{:S(2)}) collective-permute-start(bf16[2,4,16,1024]{3,2,1,0:T(8,128)(2,1)S(1)} %collective-permute-done.10), channel_id=1, source_target_pairs={{0,2},{1,3},{2,0},{3,1},{4,6},{5,7},{6,4},{7,5},{8,10},{9,11},{10,... | collective-permute-start | bytes 786440 | tf_op jit(solution)/shard_map/ppermute | solution.py:291
  31.8 14.0 %collective-permute-start.8 = (bf16[3,2,32,1024]{3,2,0,1:T(8,128)(2,1)S(1)}, bf16[3,2,32,1024]{3,2,0,1:T(8,128)(2,1)S(1)}, u32[]{:S(2)}, u32[]{:S(2)}) collective-permute-start(bf16[3,2,32,1024]{3,2,0,1:T(8,128)(2,1)S(1)} %copy.31), channel_id=1, source_target_pairs={{0,8},{8,0},{16,24},{24,16},{1,9},{9,1},{17,25},{25,17},{2,10},{10... | collective-permute-start | bytes 1179656 | tf_op jit(solution)/shard_map/ppermute | solution.py:285
  32.9 14.2 %collective-permute-start.9 = (bf16[3,2,32,1024]{3,2,0,1:T(8,128)(2,1)S(1)}, bf16[3,2,32,1024]{3,2,0,1:T(8,128)(2,1)S(1)}, u32[]{:S(2)}, u32[]{:S(2)}) collective-permute-start(bf16[3,2,32,1024]{3,2,0,1:T(8,128)(2,1)S(1)} %copy.32), channel_id=1, source_target_pairs={{0,16},{8,24},{16,0},{24,8},{1,17},{9,25},{17,1},{25,9},{2,18},{10... | collective-permute-start | bytes 1179656 | tf_op jit(solution)/shard_map/ppermute | solution.py:285
  39.7 10.3 %collective-permute-start.14 = (bf16[2,2,4,16,1024]{4,3,2,1,0:T(8,128)(2,1)S(1)}, bf16[2,2,4,16,1024]{4,3,2,1,0:T(8,128)(2,1)S(1)}, u32[]{:S(2)}, u32[]{:S(2)}) collective-permute-start(bf16[2,2,4,16,1024]{4,3,2,1,0:T(8,128)(2,1)S(1)} %pad_maximum_fusion.5.own_ref), channel_id=1, source_target_pairs={{0,1},{1,0},{2,3},{3,2},{4,5},{5,4},{6,7},{7,6},{8,9},{9,8},{10,11... | collective-permute-start | bytes 1572872 | tf_op jit(solution)/shard_map/ppermute | solution.py:288
  47.8 12.1 %collective-permute-start.12 = (bf16[3,64,1024]{2,1,0:T(8,128)(2,1)S(1)}, bf16[3,64,1024]{2,1,0:T(8,128)(2,1)S(1)}, u32[]{:S(2)}, u32[]{:S(2)}) collective-permute-start(bf16[3,64,1024]{2,1,0:T(8,128)(2,1)S(1)} %fusion.2), channel_id=1, source_target_pairs={{0,16},{8,24},{16,0},{24,8},{1,17},{9,25},{17,1},{25,9},{2,18},{10... | collective-permute-start | bytes 1179656 | tf_op jit(solution)/shard_map/ppermute | solution.py:285
  49.5 12.1 %collective-permute-start.13 = (bf16[3,64,1024]{2,1,0:T(8,128)(2,1)S(1)}, bf16[3,64,1024]{2,1,0:T(8,128)(2,1)S(1)}, u32[]{:S(2)}, u32[]{:S(2)}) collective-permute-start(bf16[3,64,1024]{2,1,0:T(8,128)(2,1)S(1)} %fusion.3), channel_id=1, source_target_pairs={{0,8},{8,0},{16,24},{24,16},{1,9},{9,1},{17,25},{25,17},{2,10},{10... | collective-permute-start | bytes 1179656 | tf_op jit(solution)/shard_map/ppermute | solution.py:285
  53.6 24.8 %collective-permute-start.17 = (bf16[3,2,64,1024]{3,2,0,1:T(8,128)(2,1)S(1)}, bf16[3,2,64,1024]{3,2,0,1:T(8,128)(2,1)S(1)}, u32[]{:S(2)}, u32[]{:S(2)}) collective-permute-start(bf16[3,2,64,1024]{3,2,0,1:T(8,128)(2,1)S(1)} %copy.36), channel_id=1, source_target_pairs={{0,8},{8,0},{16,24},{24,16},{1,9},{9,1},{17,25},{25,17},{2,10},{10... | collective-permute-start | bytes 2359304 | tf_op jit(solution)/shard_map/ppermute | solution.py:285
  55.2 23.2 %collective-permute-start.18 = (bf16[3,2,64,1024]{3,2,0,1:T(8,128)(2,1)S(1)}, bf16[3,2,64,1024]{3,2,0,1:T(8,128)(2,1)S(1)}, u32[]{:S(2)}, u32[]{:S(2)}) collective-permute-start(bf16[3,2,64,1024]{3,2,0,1:T(8,128)(2,1)S(1)} %copy.37), channel_id=1, source_target_pairs={{0,16},{8,24},{16,0},{24,8},{1,17},{9,25},{17,1},{25,9},{2,18},{10... | collective-permute-start | bytes 2359304 | tf_op jit(solution)/shard_map/ppermute | solution.py:285
  62.3 29.0 %collective-permute-start.15 = (bf16[2,64,1024]{2,1,0:T(8,128)(2,1)S(1)}, bf16[2,64,1024]{2,1,0:T(8,128)(2,1)S(1)}, u32[]{:S(2)}, u32[]{:S(2)}) collective-permute-start(bf16[2,64,1024]{2,1,0:T(8,128)(2,1)S(1)} %pad_maximum_fusion.8.refs_6_), channel_id=1, source_target_pairs={{0,16},{8,24},{16,0},{24,8},{1,17},{9,25},{17,1},{25,9},{2,18},{10... | collective-permute-start | bytes 786440 | tf_op jit(solution)/shard_map/ppermute | solution.py:285
  62.9 28.5 %collective-permute-start.16 = (bf16[2,64,1024]{2,1,0:T(8,128)(2,1)S(1)}, bf16[2,64,1024]{2,1,0:T(8,128)(2,1)S(1)}, u32[]{:S(2)}, u32[]{:S(2)}) collective-permute-start(bf16[2,64,1024]{2,1,0:T(8,128)(2,1)S(1)} %pad_maximum_fusion.9.refs_7_), channel_id=1, source_target_pairs={{0,8},{8,0},{16,24},{24,16},{1,9},{9,1},{17,25},{25,17},{2,10},{10... | collective-permute-start | bytes 786440 | tf_op jit(solution)/shard_map/ppermute | solution.py:285
  63.4 15.6 %collective-permute-start.22 = (bf16[2,16,4096]{2,1,0:T(8,128)(2,1)S(1)}, bf16[2,16,4096]{2,1,0:T(8,128)(2,1)S(1)}, u32[]{:S(2)}, u32[]{:S(2)}) collective-permute-start(bf16[2,16,4096]{2,1,0:T(8,128)(2,1)S(1)} %pad_maximum_fusion.10), channel_id=1, source_target_pairs={{0,4},{1,5},{2,6},{3,7},{4,0},{5,1},{6,2},{7,3},{8,12},{9,13},{10,... | collective-permute-start | bytes 786440 | tf_op jit(solution)/shard_map/ppermute | solution.py:291
  79.1 10.1 %collective-permute-start.19 = (bf16[3,64,1024]{2,1,0:T(8,128)(2,1)S(1)}, bf16[3,64,1024]{2,1,0:T(8,128)(2,1)S(1)}, u32[]{:S(2)}, u32[]{:S(2)}) collective-permute-start(bf16[3,64,1024]{2,1,0:T(8,128)(2,1)S(1)} %fusion.4), channel_id=1, source_target_pairs={{0,16},{8,24},{16,0},{24,8},{1,17},{9,25},{17,1},{25,9},{2,18},{10... | collective-permute-start | bytes 1179656 | tf_op jit(solution)/shard_map/ppermute | solution.py:285
  79.8 10.8 %collective-permute-start.20 = (bf16[3,64,1024]{2,1,0:T(8,128)(2,1)S(1)}, bf16[3,64,1024]{2,1,0:T(8,128)(2,1)S(1)}, u32[]{:S(2)}, u32[]{:S(2)}) collective-permute-start(bf16[3,64,1024]{2,1,0:T(8,128)(2,1)S(1)} %fusion.5), channel_id=1, source_target_pairs={{0,8},{8,0},{16,24},{24,16},{1,9},{9,1},{17,25},{25,17},{2,10},{10... | collective-permute-start | bytes 1179656 | tf_op jit(solution)/shard_map/ppermute | solution.py:285
  98.6 21.2 %collective-permute-start.31 = (bf16[2,2,96,1024]{3,2,1,0:T(8,128)(2,1)S(1)}, bf16[2,2,96,1024]{3,2,1,0:T(8,128)(2,1)S(1)}, u32[]{:S(2)}, u32[]{:S(2)}) collective-permute-start(bf16[2,2,96,1024]{3,2,1,0:T(8,128)(2,1)S(1)} %maximum_maximum_fusion.refs_0_), channel_id=1, source_target_pairs={{0,8},{8,0},{16,24},{24,16},{1,9},{9,1},{17,25},{25,17},{2,10},{10... | collective-permute-start | bytes 2359304 | tf_op jit(solution)/shard_map/ppermute | solution.py:285
  99.5 20.4 %collective-permute-start.32 = (bf16[2,2,96,1024]{3,2,1,0:T(8,128)(2,1)S(1)}, bf16[2,2,96,1024]{3,2,1,0:T(8,128)(2,1)S(1)}, u32[]{:S(2)}, u32[]{:S(2)}) collective-permute-start(bf16[2,2,96,1024]{3,2,1,0:T(8,128)(2,1)S(1)} %maximum_maximum_fusion.1.refs_2_), channel_id=1, source_target_pairs={{0,16},{8,24},{16,0},{24,8},{1,17},{9,25},{17,1},{25,9},{2,18},{10... | collective-permute-start | bytes 2359304 | tf_op jit(solution)/shard_map/ppermute | solution.py:285
  101.1 17.6 %collective-permute-start.25 = (bf16[2,5,64,128]{3,2,1,0:T(8,128)(2,1)S(1)}, bf16[2,5,64,128]{3,2,1,0:T(8,128)(2,1)S(1)}, u32[]{:S(2)}, u32[]{:S(2)}) collective-permute-start(bf16[2,5,64,128]{3,2,1,0:T(8,128)(2,1)S(1)} %fusion.30), channel_id=1, source_target_pairs={{0,8},{8,0},{16,24},{24,16},{1,9},{9,1},{17,25},{25,17},{2,10},{10... | collective-permute-start | bytes 491528 | tf_op jit(solution)/shard_map/ppermute | solution.py:285
  102.3 17.4 %collective-permute-start.26 = (bf16[2,5,64,128]{3,2,1,0:T(8,128)(2,1)S(1)}, bf16[2,5,64,128]{3,2,1,0:T(8,128)(2,1)S(1)}, u32[]{:S(2)}, u32[]{:S(2)}) collective-permute-start(bf16[2,5,64,128]{3,2,1,0:T(8,128)(2,1)S(1)} %fusion.31), channel_id=1, source_target_pairs={{0,16},{8,24},{16,0},{24,8},{1,17},{9,25},{17,1},{25,9},{2,18},{10... | collective-permute-start | bytes 491528 | tf_op jit(solution)/shard_map/ppermute | solution.py:285
  123.5 9.9 %collective-permute-start.29 = (bf16[2,2,32,1024]{3,2,1,0:T(8,128)(2,1)S(1)}, bf16[2,2,32,1024]{3,2,1,0:T(8,128)(2,1)S(1)}, u32[]{:S(2)}, u32[]{:S(2)}) collective-permute-start(bf16[2,2,32,1024]{3,2,1,0:T(8,128)(2,1)S(1)} %get-tuple-element.172.refs_0_), channel_id=1, source_target_pairs={{0,8},{8,0},{16,24},{24,16},{1,9},{9,1},{17,25},{25,17},{2,10},{10... | collective-permute-start | bytes 786440 | tf_op jit(solution)/shard_map/ppermute | solution.py:285
  125.9 13.0 %collective-permute-start.36 = (bf16[4,16,1024]{2,1,0:T(8,128)(2,1)S(1)}, bf16[4,16,1024]{2,1,0:T(8,128)(2,1)S(1)}, u32[]{:S(2)}, u32[]{:S(2)}) collective-permute-start(bf16[4,16,1024]{2,1,0:T(8,128)(2,1)S(1)} %get-tuple-element.207), channel_id=1, source_target_pairs={{0,4},{1,5},{2,6},{3,7},{4,0},{5,1},{6,2},{7,3},{8,12},{9,13},{10,... | collective-permute-start | bytes 393224 | tf_op jit(solution)/shard_map/ppermute | solution.py:291
  128.9 10.0 %collective-permute-start.37 = (bf16[4,16,1024]{2,1,0:T(8,128)(2,1)S(1)}, bf16[4,16,1024]{2,1,0:T(8,128)(2,1)S(1)}, u32[]{:S(2)}, u32[]{:S(2)}) collective-permute-start(bf16[4,16,1024]{2,1,0:T(8,128)(2,1)S(1)} %get-tuple-element.208), channel_id=1, source_target_pairs={{0,6},{1,7},{2,4},{3,5},{4,2},{5,3},{6,0},{7,1},{8,14},{9,15},{10,... | collective-permute-start | bytes 393224 | tf_op jit(solution)/shard_map/ppermute | solution.py:291
  (25 other events, 118.8 us)
where the time goes:
time: 147 us; the launch traced here: 146 us
  waiting for transfers between devices  73.3 us (50%)
  starting transfers between devices  40.2 us (27%)
  Pallas kernels  25.6 us (17%)
  other arithmetic  4.24 us (3%)
  local copies, waits for them, and re-layouts  1.64 us (1%)
    ppermute x28, waiting for transfers between devices, over_dp(): return lax.ppermute(value, 'dp', xor_perm(n_dp, mask))  57.6 us
    ppermute x28, starting transfers between devices, over_dp(): return lax.ppermute(value, 'dp', xor_perm(n_dp, mask))  30.4 us
    ppermute x9, waiting for transfers between devices, over_z(): return lax.ppermute(value, 'tensor', z_perm(n_tensor, mask))  15.6 us
    ppermute x9, starting transfers between devices, over_z(): return lax.ppermute(value, 'tensor', z_perm(n_tensor, mask))  9.49 us
    pallas_call x3, Pallas kernels, forward_partials(): pl.pallas_call(functools.partial(forward_kernel, bits), out_shape=[jax.Sh...  8.81 us
    pallas_call x2, Pallas kernels, backward_partials(): pl.pallas_call(functools.partial(backward_kernel, places), out_shape=jax....  6.36 us
    pallas_call x1, Pallas kernels, window_deltas(): pl.pallas_call(functools.partial(delta_kernel, n_dp, len(hiddens)), out_s...  5.11 us
    pallas_call x1, Pallas kernels, in_vmem(): pl.pallas_call(load_kernel, out_shape=[pltpu.VMEM(w.shape, w.dtype) for w...  4.69 us
  transfers between devices with their start and end apart: 43, of which 21 were waited for; matrix products, arithmetic and copies ran while one was open for 3% of the time, Pallas kernels for 15%

commit v1 on v0

--- a/solution.py
+++ b/solution.py
@@ -180,11 +180,7 @@
         out_specs=[vmem] * 2 * len(bits),
         scratch_shapes=[pltpu.VMEM((2, windows * count, width), own.dtype)],
         compiler_params=pltpu.CompilerParams(vmem_limit_bytes=16 << 20),
-        cost_estimate=SMALL if chips > 1 else pl.CostEstimate(
-            flops=1*6 * windows * count * width * gate_weight.shape[1],
-            bytes_accessed=3 * width * gate_weight.shape[1],
-            transcendentals=0,
-        ),
+        cost_estimate=SMALL,
     )(own, other, gate_weight, up_weight, down_weight)
     return outs[::2], outs[1::2]
 
@@ -302,6 +298,7 @@
         low = mask & -mask if mask else n_z
         for step in range(low.bit_length() - 1):
             hop(held, mask | 1 << step)
+        chain.append(held[mask])
 
     def swap(k):
         got = ordered(*[held[mask] for mask in masks[k]])
@@ -514,29 +511,29 @@
     for mask in masks["near"][1::2]:
         relay(held, mask)
     swap("near")
-    for mask in masks[1][::2]:
-        relay(held, mask)
     forward("near")
     send("near", 0)
     take("own", 0)
-    swap(1)
+    for mask in masks[1][::2]:
+        relay(held, mask)
     take("near", 0)
     merge()
-    send(0, 1)
-    forward(1)
-    send(1, 0)
+    for s in range(1, stages - 1):
+        send(0, s)
+        if s == stages - 2:
+            swap(1)
+            forward(1)
+            send(1, 0)
+        take(0, s)
     window_rows(0)
     hops = iter(range(1, n_z))
-    for s in range(2, stages - 1):
-        take(0, s - 1)
-        send(0, s)
+    for s in range(1, stages - 2):
         window_rows(next(hops))
-        take(1, s - 2)
-        send(1, s - 1)
+        take(1, s - 1)
+        send(1, s)
     for mask in hops:
         window_rows(mask)
     take(1, stages - 3)
-    take(0, stages - 2)
     send(1, stages - 2)
     delta_terms()
     send("delta", 0)

time: 147 us -> 150 us (1.020)
  starting transfers between devices: 40.2 us -> 47.2 us
  waiting for transfers between devices: 73.3 us -> 69.1 us
    ppermute x28, waiting for transfers between devices: 57.6 us -> 43.4 us  [over_dp(): return lax.ppermute(value, 'dp', xor_perm(n_dp, mask))]
    ppermute x9, waiting for transfers between devices: 15.6 us -> 24.9 us  [over_z(): return lax.ppermute(value, 'tensor', z_perm(n_tensor, mask))]
    ppermute x9, starting transfers between devices: 9.49 us -> 14 us  [over_z(): return lax.ppermute(value, 'tensor', z_perm(n_tensor, mask))]
    ppermute x28, starting transfers between devices: 30.4 us -> 32.9 us  [over_dp(): return lax.ppermute(value, 'dp', xor_perm(n_dp, mask))]
  transfers between devices with their start and end apart: 43 -> 43, of which waited for: 21 -> 23; matrix products, arithmetic and copies ran while one was open for 3% -> 3% of each run, Pallas kernels for 15% -> 14%
where the time goes in v1:
time: 150 us; the launch traced here: 149 us
  waiting for transfers between devices  69.1 us (46%)
  starting transfers between devices  47.2 us (31%)
  Pallas kernels  25.6 us (17%)
  other arithmetic  4.23 us (3%)
  local copies, waits for them, and re-layouts  1.64 us (1%)
    ppermute x28, waiting for transfers between devices, over_dp(): return lax.ppermute(value, 'dp', xor_perm(n_dp, mask))  43.4 us
    ppermute x28, starting transfers between devices, over_dp(): return lax.ppermute(value, 'dp', xor_perm(n_dp, mask))  32.9 us
    ppermute x9, waiting for transfers between devices, over_z(): return lax.ppermute(value, 'tensor', z_perm(n_tensor, mask))  24.9 us
    ppermute x9, starting transfers between devices, over_z(): return lax.ppermute(value, 'tensor', z_perm(n_tensor, mask))  14 us
    pallas_call x3, Pallas kernels, forward_partials(): pl.pallas_call(functools.partial(forward_kernel, bits), out_shape=[jax.Sh...  8.81 us
    pallas_call x2, Pallas kernels, backward_partials(): pl.pallas_call(functools.partial(backward_kernel, places), out_shape=jax....  6.36 us
    pallas_call x1, Pallas kernels, window_deltas(): pl.pallas_call(functools.partial(delta_kernel, n_dp, len(hiddens)), out_s...  5.11 us
    pallas_call x1, Pallas kernels, in_vmem(): pl.pallas_call(load_kernel, out_shape=[pltpu.VMEM(w.shape, w.dtype) for w...  4.69 us
  transfers between devices with their start and end apart: 43, of which 23 were waited for; matrix products, arithmetic and copies ran while one was open for 3% of the time, Pallas kernels for 14%

profile of v1, /device:TPU:0, one launch (start us, length us, event | category | flops | bytes accessed | tf_op | source)
XLA Modules:
  0.0 149.2 jit_solution(9747873050156399005)
XLA Ops:
  1.6 3.0 %collective-permute-start = (bf16[2,16,1024]{2,1,0:T(8,128)(2,1)S(1)}, bf16[2,16,1024]{2,1,0:T(8,128)(2,1)S(1)}, u32[]{:S(2)}, u32[]{:S(2)}) collective-permute-start(bf16[2,16,1024]{2,1,0:T(8,128)(2,1)S(1)} %pad_maximum_fusion.14), channel_id=1, source_target_pairs={{0,8},{8,0},{16,24},{24,16},{1,9},{9,1},{17,25},{25,17},{2,10},{10... | collective-permute-start | bytes 196616 | tf_op jit(solution)/shard_map/ppermute | solution.py:281
  6.2 4.7 %shard_map.104 = (bf16[1024,2048]{1,0:T(8,128)(2,1)S(1)}, bf16[1024,2048]{1,0:T(8,128)(2,1)S(1)}, bf16[2048,1024]{1,0:T(8,128)(2,1)S(1)}) custom-call(bf16[1024,2048]{1,0:T(8,128)(2,1)} %refs_0_.1, bf16[1024,2048]{1,0:T(8,128)(2,1)} %refs_1_.1, bf16[2048,1024]{1,0:T(8,128)(2,1)} %refs_2_.1), custom_call_target="tpu_custom_call" | custom-call | flops 1 | bytes 1 | tf_op jit(solution)/shard_map/pallas_call | solution.py:125
  11.5 1.7 %collective-permute-start.6 = (bf16[2,4,16,1024]{3,2,1,0:T(8,128)(2,1)S(1)}, bf16[2,4,16,1024]{3,2,1,0:T(8,128)(2,1)S(1)}, u32[]{:S(2)}, u32[]{:S(2)}) collective-permute-start(bf16[2,4,16,1024]{3,2,1,0:T(8,128)(2,1)S(1)} %pad_maximum_fusion.7), channel_id=1, source_target_pairs={{0,2},{1,3},{2,0},{3,1},{4,6},{5,7},{6,4},{7,5},{8,10},{9,11},{10,... | collective-permute-start | bytes 786440 | tf_op jit(solution)/shard_map/ppermute | solution.py:287
  13.2 2.7 %shard_map.105 = (bf16[3,2,32,1024]{3,2,1,0:T(8,128)(2,1)S(1)}, bf16[3,2,32,1024]{3,2,1,0:T(8,128)(2,1)S(1)}, bf16[3,2,32,1024]{3,2,1,0:T(8,128)(2,1)S(1)}, bf16[3,2,32,1024]{3,2,1,0:T(8,128)(2,1)S(1)}) custom-call(bf16[1,2,4,16,1024]{4,3,2,1,0:T(8,128)(2,1)S(1)} %bitcast.193, bf16[1,2,4,16,1024]{4,3,2,1,0:T(8,128)(2,1)S(1)} %collective-permute-done.3.other_ref, ...), custom_call_target="tpu_custom_call" | custom-call | flops 1 | bytes 1 | tf_op jit(solution)/shard_map/pallas_call | solution.py:176
  17.5 1.6 %collective-permute-start.5 = (bf16[3,2,32,1024]{3,2,0,1:T(8,128)(2,1)S(1)}, bf16[3,2,32,1024]{3,2,0,1:T(8,128)(2,1)S(1)}, u32[]{:S(2)}, u32[]{:S(2)}) collective-permute-start(bf16[3,2,32,1024]{3,2,0,1:T(8,128)(2,1)S(1)} %copy.29), channel_id=1, source_target_pairs={{0,16},{8,24},{16,0},{24,8},{1,17},{9,25},{17,1},{25,9},{2,18},{10... | collective-permute-start | bytes 1179656 | tf_op jit(solution)/shard_map/ppermute | solution.py:281
  20.2 2.6 %collective-permute-start.10 = (bf16[2,4,16,1024]{3,2,1,0:T(8,128)(2,1)S(1)}, bf16[2,4,16,1024]{3,2,1,0:T(8,128)(2,1)S(1)}, u32[]{:S(2)}, u32[]{:S(2)}) collective-permute-start(bf16[2,4,16,1024]{3,2,1,0:T(8,128)(2,1)S(1)} %pad_maximum_fusion.7), channel_id=1, source_target_pairs={{0,4},{1,5},{2,6},{3,7},{4,0},{5,1},{6,2},{7,3},{8,12},{9,13},{10,... | collective-permute-start | bytes 786440 | tf_op jit(solution)/shard_map/ppermute | solution.py:287
  22.9 2.7 %shard_map.106 = (bf16[3,2,32,1024]{3,2,1,0:T(8,128)(2,1)S(1)}, bf16[3,2,32,1024]{3,2,1,0:T(8,128)(2,1)S(1)}, bf16[3,2,32,1024]{3,2,1,0:T(8,128)(2,1)S(1)}, bf16[3,2,32,1024]{3,2,1,0:T(8,128)(2,1)S(1)}) custom-call(bf16[1,2,4,16,1024]{4,3,2,1,0:T(8,128)(2,1)S(1)} %bitcast.195, bf16[1,2,4,16,1024]{4,3,2,1,0:T(8,128)(2,1)S(1)} %collective-permute-done.7.other_ref, ...), custom_call_target="tpu_custom_call" | custom-call | flops 1 | bytes 1 | tf_op jit(solution)/shard_map/pallas_call | solution.py:176
  27.2 1.6 %collective-permute-start.9 = (bf16[3,2,32,1024]{3,2,0,1:T(8,128)(2,1)S(1)}, bf16[3,2,32,1024]{3,2,0,1:T(8,128)(2,1)S(1)}, u32[]{:S(2)}, u32[]{:S(2)}) collective-permute-start(bf16[3,2,32,1024]{3,2,0,1:T(8,128)(2,1)S(1)} %copy.32), channel_id=1, source_target_pairs={{0,16},{8,24},{16,0},{24,8},{1,17},{9,25},{17,1},{25,9},{2,18},{10... | collective-permute-start | bytes 1179656 | tf_op jit(solution)/shard_map/ppermute | solution.py:281
  29.0 6.5 %collective-permute-done.10 = bf16[2,4,16,1024]{3,2,1,0:T(8,128)(2,1)S(1)} collective-permute-done((bf16[2,4,16,1024]{3,2,1,0:T(8,128)(2,1)S(1)}, bf16[2,4,16,1024]{3,2,1,0:T(8,128)(2,1)S(1)}, u32[]{:S(2)}, u32[]{:S(2)}) %collective-permute-start.10) | collective-permute-done | bytes 262176 | tf_op jit(solution)/shard_map/ppermute | solution.py:287
  42.7 6.4 %collective-permute-done.11 = bf16[3,64,1024]{2,1,0:T(8,128)(2,1)S(1)} collective-permute-done((bf16[3,64,1024]{2,1,0:T(8,128)(2,1)S(1)}, bf16[3,64,1024]{2,1,0:T(8,128)(2,1)S(1)}, u32[]{:S(2)}, u32[]{:S(2)}) %collective-permute-start.11) | collective-permute-done | bytes 393248 | tf_op jit(solution)/shard_map/ppermute | solution.py:281
  53.2 3.5 %shard_map.107 = (bf16[3,2,64,1024]{3,2,1,0:T(8,128)(2,1)S(1)}, bf16[3,2,64,1024]{3,2,1,0:T(8,128)(2,1)S(1)}, bf16[3,2,64,1024]{3,2,1,0:T(8,128)(2,1)S(1)}, bf16[3,2,64,1024]{3,2,1,0:T(8,128)(2,1)S(1)}) custom-call(bf16[2,2,4,16,1024]{4,3,2,1,0:T(8,128)(2,1)S(1)} %pad_maximum_fusion.5.own_ref, ...), custom_call_target="tpu_custom_call" | custom-call | flops 1 | bytes 1 | tf_op jit(solution)/shard_map/pallas_call | solution.py:176
  61.0 1.6 %collective-permute-start.17 = (bf16[2,16,4096]{2,1,0:T(8,128)(2,1)S(1)}, bf16[2,16,4096]{2,1,0:T(8,128)(2,1)S(1)}, u32[]{:S(2)}, u32[]{:S(2)}) collective-permute-start(bf16[2,16,4096]{2,1,0:T(8,128)(2,1)S(1)} %pad_maximum_fusion.10), channel_id=1, source_target_pairs={{0,2},{1,3},{2,0},{3,1},{4,6},{5,7},{6,4},{7,5},{8,10},{9,11},{10,... | collective-permute-start | bytes 786440 | tf_op jit(solution)/shard_map/ppermute | solution.py:287
  62.6 5.4 %collective-permute-done.17 = bf16[2,16,4096]{2,1,0:T(8,128)(2,1)S(1)} collective-permute-done((bf16[2,16,4096]{2,1,0:T(8,128)(2,1)S(1)}, bf16[2,16,4096]{2,1,0:T(8,128)(2,1)S(1)}, u32[]{:S(2)}, u32[]{:S(2)}) %collective-permute-start.17) | collective-permute-done | bytes 262176 | tf_op jit(solution)/shard_map/ppermute | solution.py:287
  69.4 7.7 %collective-permute-done.19 = bf16[3,2,64,1024]{3,2,0,1:T(8,128)(2,1)S(1)} collective-permute-done((bf16[3,2,64,1024]{3,2,0,1:T(8,128)(2,1)S(1)}, bf16[3,2,64,1024]{3,2,0,1:T(8,128)(2,1)S(1)}, u32[]{:S(2)}, u32[]{:S(2)}) %collective-permute-start.19) | collective-permute-done | bytes 786464 | tf_op jit(solution)/shard_map/ppermute | solution.py:281
  77.7 2.9 %collective-permute-done.18 = bf16[2,16,4096]{2,1,0:T(8,128)(2,1)S(1)} collective-permute-done((bf16[2,16,4096]{2,1,0:T(8,128)(2,1)S(1)}, bf16[2,16,4096]{2,1,0:T(8,128)(2,1)S(1)}, u32[]{:S(2)}, u32[]{:S(2)}) %collective-permute-start.18) | collective-permute-done | bytes 262176 | tf_op jit(solution)/shard_map/ppermute | solution.py:287
  82.6 5.1 %collective-permute-done.21 = bf16[2,16,4096]{2,1,0:T(8,128)(2,1)S(1)} collective-permute-done((bf16[2,16,4096]{2,1,0:T(8,128)(2,1)S(1)}, bf16[2,16,4096]{2,1,0:T(8,128)(2,1)S(1)}, u32[]{:S(2)}, u32[]{:S(2)}) %collective-permute-start.21) | collective-permute-done | bytes 262176 | tf_op jit(solution)/shard_map/ppermute | solution.py:287
  87.9 3.0 %collective-permute-done.23 = bf16[3,64,1024]{2,1,0:T(8,128)(2,1)S(1)} collective-permute-done((bf16[3,64,1024]{2,1,0:T(8,128)(2,1)S(1)}, bf16[3,64,1024]{2,1,0:T(8,128)(2,1)S(1)}, u32[]{:S(2)}, u32[]{:S(2)}) %collective-permute-start.23) | collective-permute-done | bytes 393248 | tf_op jit(solution)/shard_map/ppermute | solution.py:281
  94.8 5.1 %shard_map.108 = f32[20,128,128]{2,1,0:T(8,128)S(1)} custom-call(s32[1]{0:T(128)} %bitcast.me_ref, s32[20]{0:T(128)S(1)} %copy-done, s32[20]{0:T(128)S(1)} %copy-done.1, s32[20]{0:T(128)S(1)} %copy-done.2, s32[20]{0:T(128)S(1)} %bitcast.196, bf16[2,4,16,4096]{3,2,1,0:T(8,128)(2,1)S(1)} %pad_maximum_fusion.2.refs_0_, ...), custom_call_target="tpu_custom_call" | custom-call | flops 1 | bytes 1 | tf_op jit(solution)/shard_map/pallas_call | solution.py:94
  104.5 16.4 %collective-permute-done.25 = bf16[2,5,64,128]{3,2,1,0:T(8,128)(2,1)S(1)} collective-permute-done((bf16[2,5,64,128]{3,2,1,0:T(8,128)(2,1)S(1)}, bf16[2,5,64,128]{3,2,1,0:T(8,128)(2,1)S(1)}, u32[]{:S(2)}, u32[]{:S(2)}) %collective-permute-start.25) | collective-permute-done | bytes 163872 | tf_op jit(solution)/shard_map/ppermute | solution.py:281
  121.3 3.5 %shard_map.109 = f32[384,1024]{1,0:T(8,128)S(1)} custom-call(bf16[2,2,96,1024]{3,2,1,0:T(8,128)(2,1)S(1)} %maximum_maximum_fusion.refs_0_, bf16[2,2,96,1024]{3,2,1,0:T(8,128)(2,1)S(1)} %collective-permute-done.31.refs_1_, bf16[2,2,96,1024]{3,2,1,0:T(8,128)(2,1)S(1)} %maximum_maximum_fusion.1.refs_2_, ...), custom_call_target="tpu_custom_call" | custom-call | flops 1 | bytes 1 | tf_op jit(solution)/shard_map/pallas_call | solution.py:214
  128.0 3.7 %collective-permute-start.36 = (bf16[4,16,1024]{2,1,0:T(8,128)(2,1)S(1)}, bf16[4,16,1024]{2,1,0:T(8,128)(2,1)S(1)}, u32[]{:S(2)}, u32[]{:S(2)}) collective-permute-start(bf16[4,16,1024]{2,1,0:T(8,128)(2,1)S(1)} %get-tuple-element.207), channel_id=1, source_target_pairs={{0,4},{1,5},{2,6},{3,7},{4,0},{5,1},{6,2},{7,3},{8,12},{9,13},{10,... | collective-permute-start | bytes 393224 | tf_op jit(solution)/shard_map/ppermute | solution.py:287
  132.6 3.0 %collective-permute-done.34 = bf16[4,16,1024]{2,1,0:T(8,128)(2,1)S(1)} collective-permute-done((bf16[4,16,1024]{2,1,0:T(8,128)(2,1)S(1)}, bf16[4,16,1024]{2,1,0:T(8,128)(2,1)S(1)}, u32[]{:S(2)}, u32[]{:S(2)}) %collective-permute-start.34) | collective-permute-done | bytes 131104 | tf_op jit(solution)/shard_map/ppermute | solution.py:287
  135.6 2.9 %shard_map.110 = f32[128,1024]{1,0:T(8,128)S(1)} custom-call(bf16[2,2,32,1024]{3,2,1,0:T(8,128)(2,1)S(1)} %get-tuple-element.172.refs_0_, bf16[2,2,32,1024]{3,2,1,0:T(8,128)(2,1)S(1)} %collective-permute-done.29.refs_1_, bf16[2,2,32,1024]{3,2,1,0:T(8,128)(2,1)S(1)} %get-tuple-element.173.refs_2_, ...), custom_call_target="tpu_custom_call" | custom-call | flops 1 | bytes 1 | tf_op jit(solution)/shard_map/pallas_call | solution.py:214
  146.8 1.7 %collective-permute-done.40.refs_3_ = bf16[16,1024]{1,0:T(8,128)(2,1)S(1)} collective-permute-done((bf16[16,1024]{1,0:T(8,128)(2,1)S(1)}, bf16[16,1024]{1,0:T(8,128)(2,1)S(1)}, u32[]{:S(2)}, u32[]{:S(2)}) %collective-permute-start.40) | collective-permute-done | bytes 32800 | tf_op jit(solution)/shard_map/ppermute | solution.py:281
  (147 shorter events, 48.9 us)
Async XLA Ops:
  1.6 9.4 %collective-permute-start = (bf16[2,16,1024]{2,1,0:T(8,128)(2,1)S(1)}, bf16[2,16,1024]{2,1,0:T(8,128)(2,1)S(1)}, u32[]{:S(2)}, u32[]{:S(2)}) collective-permute-start(bf16[2,16,1024]{2,1,0:T(8,128)(2,1)S(1)} %pad_maximum_fusion.14), channel_id=1, source_target_pairs={{0,8},{8,0},{16,24},{24,16},{1,9},{9,1},{17,25},{25,17},{2,10},{10... | collective-permute-start | bytes 196616 | tf_op jit(solution)/shard_map/ppermute | solution.py:281
  15.9 12.9 %collective-permute-start.4 = (bf16[3,2,32,1024]{3,2,0,1:T(8,128)(2,1)S(1)}, bf16[3,2,32,1024]{3,2,0,1:T(8,128)(2,1)S(1)}, u32[]{:S(2)}, u32[]{:S(2)}) collective-permute-start(bf16[3,2,32,1024]{3,2,0,1:T(8,128)(2,1)S(1)} %copy.28), channel_id=1, source_target_pairs={{0,8},{8,0},{16,24},{24,16},{1,9},{9,1},{17,25},{25,17},{2,10},{10... | collective-permute-start | bytes 1179656 | tf_op jit(solution)/shard_map/ppermute | solution.py:281
  17.5 11.3 %collective-permute-start.5 = (bf16[3,2,32,1024]{3,2,0,1:T(8,128)(2,1)S(1)}, bf16[3,2,32,1024]{3,2,0,1:T(8,128)(2,1)S(1)}, u32[]{:S(2)}, u32[]{:S(2)}) collective-permute-start(bf16[3,2,32,1024]{3,2,0,1:T(8,128)(2,1)S(1)} %copy.29), channel_id=1, source_target_pairs={{0,16},{8,24},{16,0},{24,8},{1,17},{9,25},{17,1},{25,9},{2,18},{10... | collective-permute-start | bytes 1179656 | tf_op jit(solution)/shard_map/ppermute | solution.py:281
  20.2 15.2 %collective-permute-start.10 = (bf16[2,4,16,1024]{3,2,1,0:T(8,128)(2,1)S(1)}, bf16[2,4,16,1024]{3,2,1,0:T(8,128)(2,1)S(1)}, u32[]{:S(2)}, u32[]{:S(2)}) collective-permute-start(bf16[2,4,16,1024]{3,2,1,0:T(8,128)(2,1)S(1)} %pad_maximum_fusion.7), channel_id=1, source_target_pairs={{0,4},{1,5},{2,6},{3,7},{4,0},{5,1},{6,2},{7,3},{8,12},{9,13},{10,... | collective-permute-start | bytes 786440 | tf_op jit(solution)/shard_map/ppermute | solution.py:287
  25.6 11.3 %collective-permute-start.8 = (bf16[3,2,32,1024]{3,2,0,1:T(8,128)(2,1)S(1)}, bf16[3,2,32,1024]{3,2,0,1:T(8,128)(2,1)S(1)}, u32[]{:S(2)}, u32[]{:S(2)}) collective-permute-start(bf16[3,2,32,1024]{3,2,0,1:T(8,128)(2,1)S(1)} %copy.31), channel_id=1, source_target_pairs={{0,8},{8,0},{16,24},{24,16},{1,9},{9,1},{17,25},{25,17},{2,10},{10... | collective-permute-start | bytes 1179656 | tf_op jit(solution)/shard_map/ppermute | solution.py:281
  27.2 11.0 %collective-permute-start.9 = (bf16[3,2,32,1024]{3,2,0,1:T(8,128)(2,1)S(1)}, bf16[3,2,32,1024]{3,2,0,1:T(8,128)(2,1)S(1)}, u32[]{:S(2)}, u32[]{:S(2)}) collective-permute-start(bf16[3,2,32,1024]{3,2,0,1:T(8,128)(2,1)S(1)} %copy.32), channel_id=1, source_target_pairs={{0,16},{8,24},{16,0},{24,8},{1,17},{9,25},{17,1},{25,9},{2,18},{10... | collective-permute-start | bytes 1179656 | tf_op jit(solution)/shard_map/ppermute | solution.py:281
  38.9 10.2 %collective-permute-start.11 = (bf16[3,64,1024]{2,1,0:T(8,128)(2,1)S(1)}, bf16[3,64,1024]{2,1,0:T(8,128)(2,1)S(1)}, u32[]{:S(2)}, u32[]{:S(2)}) collective-permute-start(bf16[3,64,1024]{2,1,0:T(8,128)(2,1)S(1)} %fusion.2), channel_id=1, source_target_pairs={{0,16},{8,24},{16,0},{24,8},{1,17},{9,25},{17,1},{25,9},{2,18},{10... | collective-permute-start | bytes 1179656 | tf_op jit(solution)/shard_map/ppermute | solution.py:281
  40.5 9.9 %collective-permute-start.12 = (bf16[3,64,1024]{2,1,0:T(8,128)(2,1)S(1)}, bf16[3,64,1024]{2,1,0:T(8,128)(2,1)S(1)}, u32[]{:S(2)}, u32[]{:S(2)}) collective-permute-start(bf16[3,64,1024]{2,1,0:T(8,128)(2,1)S(1)} %fusion.3), channel_id=1, source_target_pairs={{0,8},{8,0},{16,24},{24,16},{1,9},{9,1},{17,25},{25,17},{2,10},{10... | collective-permute-start | bytes 1179656 | tf_op jit(solution)/shard_map/ppermute | solution.py:281
  41.1 10.0 %collective-permute-start.15 = (bf16[2,4,16,1024]{3,2,1,0:T(8,128)(2,1)S(1)}, bf16[2,4,16,1024]{3,2,1,0:T(8,128)(2,1)S(1)}, u32[]{:S(2)}, u32[]{:S(2)}) collective-permute-start(bf16[2,4,16,1024]{3,2,1,0:T(8,128)(2,1)S(1)} %collective-permute-done.10), channel_id=1, source_target_pairs={{0,2},{1,3},{2,0},{3,1},{4,6},{5,7},{6,4},{7,5},{8,10},{9,11},{10,... | collective-permute-start | bytes 786440 | tf_op jit(solution)/shard_map/ppermute | solution.py:287
  51.3 8.7 %collective-permute-start.13 = (bf16[2,64,1024]{2,1,0:T(8,128)(2,1)S(1)}, bf16[2,64,1024]{2,1,0:T(8,128)(2,1)S(1)}, u32[]{:S(2)}, u32[]{:S(2)}) collective-permute-start(bf16[2,64,1024]{2,1,0:T(8,128)(2,1)S(1)} %pad_maximum_fusion.8.refs_6_), channel_id=1, source_target_pairs={{0,16},{8,24},{16,0},{24,8},{1,17},{9,25},{17,1},{25,9},{2,18},{10... | collective-permute-start | bytes 786440 | tf_op jit(solution)/shard_map/ppermute | solution.py:281
  51.9 9.0 %collective-permute-start.14 = (bf16[2,64,1024]{2,1,0:T(8,128)(2,1)S(1)}, bf16[2,64,1024]{2,1,0:T(8,128)(2,1)S(1)}, u32[]{:S(2)}, u32[]{:S(2)}) collective-permute-start(bf16[2,64,1024]{2,1,0:T(8,128)(2,1)S(1)} %pad_maximum_fusion.9.refs_7_), channel_id=1, source_target_pairs={{0,8},{8,0},{16,24},{24,16},{1,9},{9,1},{17,25},{25,17},{2,10},{10... | collective-permute-start | bytes 786440 | tf_op jit(solution)/shard_map/ppermute | solution.py:281
  56.7 20.4 %collective-permute-start.19 = (bf16[3,2,64,1024]{3,2,0,1:T(8,128)(2,1)S(1)}, bf16[3,2,64,1024]{3,2,0,1:T(8,128)(2,1)S(1)}, u32[]{:S(2)}, u32[]{:S(2)}) collective-permute-start(bf16[3,2,64,1024]{3,2,0,1:T(8,128)(2,1)S(1)} %copy.36), channel_id=1, source_target_pairs={{0,8},{8,0},{16,24},{24,16},{1,9},{9,1},{17,25},{25,17},{2,10},{10... | collective-permute-start | bytes 2359304 | tf_op jit(solution)/shard_map/ppermute | solution.py:281
  57.6 19.5 %collective-permute-start.20 = (bf16[3,2,64,1024]{3,2,0,1:T(8,128)(2,1)S(1)}, bf16[3,2,64,1024]{3,2,0,1:T(8,128)(2,1)S(1)}, u32[]{:S(2)}, u32[]{:S(2)}) collective-permute-start(bf16[3,2,64,1024]{3,2,0,1:T(8,128)(2,1)S(1)} %copy.37), channel_id=1, source_target_pairs={{0,16},{8,24},{16,0},{24,8},{1,17},{9,25},{17,1},{25,9},{2,18},{10... | collective-permute-start | bytes 2359304 | tf_op jit(solution)/shard_map/ppermute | solution.py:281
  68.0 12.6 %collective-permute-start.18 = (bf16[2,16,4096]{2,1,0:T(8,128)(2,1)S(1)}, bf16[2,16,4096]{2,1,0:T(8,128)(2,1)S(1)}, u32[]{:S(2)}, u32[]{:S(2)}) collective-permute-start(bf16[2,16,4096]{2,1,0:T(8,128)(2,1)S(1)} %pad_maximum_fusion.10), channel_id=1, source_target_pairs={{0,4},{1,5},{2,6},{3,7},{4,0},{5,1},{6,2},{7,3},{8,12},{9,13},{10,... | collective-permute-start | bytes 786440 | tf_op jit(solution)/shard_map/ppermute | solution.py:287
  80.6 10.2 %collective-permute-start.23 = (bf16[3,64,1024]{2,1,0:T(8,128)(2,1)S(1)}, bf16[3,64,1024]{2,1,0:T(8,128)(2,1)S(1)}, u32[]{:S(2)}, u32[]{:S(2)}) collective-permute-start(bf16[3,64,1024]{2,1,0:T(8,128)(2,1)S(1)} %fusion.4), channel_id=1, source_target_pairs={{0,16},{8,24},{16,0},{24,8},{1,17},{9,25},{17,1},{25,9},{2,18},{10... | collective-permute-start | bytes 1179656 | tf_op jit(solution)/shard_map/ppermute | solution.py:281
  82.0 9.7 %collective-permute-start.24 = (bf16[3,64,1024]{2,1,0:T(8,128)(2,1)S(1)}, bf16[3,64,1024]{2,1,0:T(8,128)(2,1)S(1)}, u32[]{:S(2)}, u32[]{:S(2)}) collective-permute-start(bf16[3,64,1024]{2,1,0:T(8,128)(2,1)S(1)} %fusion.5), channel_id=1, source_target_pairs={{0,8},{8,0},{16,24},{24,16},{1,9},{9,1},{17,25},{25,17},{2,10},{10... | collective-permute-start | bytes 1179656 | tf_op jit(solution)/shard_map/ppermute | solution.py:281
  100.1 21.2 %collective-permute-start.31 = (bf16[2,2,96,1024]{3,2,1,0:T(8,128)(2,1)S(1)}, bf16[2,2,96,1024]{3,2,1,0:T(8,128)(2,1)S(1)}, u32[]{:S(2)}, u32[]{:S(2)}) collective-permute-start(bf16[2,2,96,1024]{3,2,1,0:T(8,128)(2,1)S(1)} %maximum_maximum_fusion.refs_0_), channel_id=1, source_target_pairs={{0,8},{8,0},{16,24},{24,16},{1,9},{9,1},{17,25},{25,17},{2,10},{10... | collective-permute-start | bytes 2359304 | tf_op jit(solution)/shard_map/ppermute | solution.py:281
  101.2 20.1 %collective-permute-start.32 = (bf16[2,2,96,1024]{3,2,1,0:T(8,128)(2,1)S(1)}, bf16[2,2,96,1024]{3,2,1,0:T(8,128)(2,1)S(1)}, u32[]{:S(2)}, u32[]{:S(2)}) collective-permute-start(bf16[2,2,96,1024]{3,2,1,0:T(8,128)(2,1)S(1)} %maximum_maximum_fusion.1.refs_2_), channel_id=1, source_target_pairs={{0,16},{8,24},{16,0},{24,8},{1,17},{9,25},{17,1},{25,9},{2,18},{10... | collective-permute-start | bytes 2359304 | tf_op jit(solution)/shard_map/ppermute | solution.py:281
  102.4 18.5 %collective-permute-start.25 = (bf16[2,5,64,128]{3,2,1,0:T(8,128)(2,1)S(1)}, bf16[2,5,64,128]{3,2,1,0:T(8,128)(2,1)S(1)}, u32[]{:S(2)}, u32[]{:S(2)}) collective-permute-start(bf16[2,5,64,128]{3,2,1,0:T(8,128)(2,1)S(1)} %fusion.30), channel_id=1, source_target_pairs={{0,8},{8,0},{16,24},{24,16},{1,9},{9,1},{17,25},{25,17},{2,10},{10... | collective-permute-start | bytes 491528 | tf_op jit(solution)/shard_map/ppermute | solution.py:281
  103.4 17.7 %collective-permute-start.26 = (bf16[2,5,64,128]{3,2,1,0:T(8,128)(2,1)S(1)}, bf16[2,5,64,128]{3,2,1,0:T(8,128)(2,1)S(1)}, u32[]{:S(2)}, u32[]{:S(2)}) collective-permute-start(bf16[2,5,64,128]{3,2,1,0:T(8,128)(2,1)S(1)} %fusion.31), channel_id=1, source_target_pairs={{0,16},{8,24},{16,0},{24,8},{1,17},{9,25},{17,1},{25,9},{2,18},{10... | collective-permute-start | bytes 491528 | tf_op jit(solution)/shard_map/ppermute | solution.py:281
  124.9 10.6 %collective-permute-start.29 = (bf16[2,2,32,1024]{3,2,1,0:T(8,128)(2,1)S(1)}, bf16[2,2,32,1024]{3,2,1,0:T(8,128)(2,1)S(1)}, u32[]{:S(2)}, u32[]{:S(2)}) collective-permute-start(bf16[2,2,32,1024]{3,2,1,0:T(8,128)(2,1)S(1)} %get-tuple-element.172.refs_0_), channel_id=1, source_target_pairs={{0,8},{8,0},{16,24},{24,16},{1,9},{9,1},{17,25},{25,17},{2,10},{10... | collective-permute-start | bytes 786440 | tf_op jit(solution)/shard_map/ppermute | solution.py:281
  126.5 9.1 %collective-permute-start.30 = (bf16[2,2,32,1024]{3,2,1,0:T(8,128)(2,1)S(1)}, bf16[2,2,32,1024]{3,2,1,0:T(8,128)(2,1)S(1)}, u32[]{:S(2)}, u32[]{:S(2)}) collective-permute-start(bf16[2,2,32,1024]{3,2,1,0:T(8,128)(2,1)S(1)} %get-tuple-element.173.refs_2_), channel_id=1, source_target_pairs={{0,16},{8,24},{16,0},{24,8},{1,17},{9,25},{17,1},{25,9},{2,18},{10... | collective-permute-start | bytes 786440 | tf_op jit(solution)/shard_map/ppermute | solution.py:281
  128.0 12.6 %collective-permute-start.36 = (bf16[4,16,1024]{2,1,0:T(8,128)(2,1)S(1)}, bf16[4,16,1024]{2,1,0:T(8,128)(2,1)S(1)}, u32[]{:S(2)}, u32[]{:S(2)}) collective-permute-start(bf16[4,16,1024]{2,1,0:T(8,128)(2,1)S(1)} %get-tuple-element.207), channel_id=1, source_target_pairs={{0,4},{1,5},{2,6},{3,7},{4,0},{5,1},{6,2},{7,3},{8,12},{9,13},{10,... | collective-permute-start | bytes 393224 | tf_op jit(solution)/shard_map/ppermute | solution.py:287
  131.7 9.9 %collective-permute-start.37 = (bf16[4,16,1024]{2,1,0:T(8,128)(2,1)S(1)}, bf16[4,16,1024]{2,1,0:T(8,128)(2,1)S(1)}, u32[]{:S(2)}, u32[]{:S(2)}) collective-permute-start(bf16[4,16,1024]{2,1,0:T(8,128)(2,1)S(1)} %get-tuple-element.208), channel_id=1, source_target_pairs={{0,6},{1,7},{2,4},{3,5},{4,2},{5,3},{6,0},{7,1},{8,14},{9,15},{10,... | collective-permute-start | bytes 393224 | tf_op jit(solution)/shard_map/ppermute | solution.py:287
  (25 other events, 118.1 us)

commit v2 on v1

--- a/solution.py
+++ b/solution.py
@@ -470,15 +470,17 @@
         done(total)
         return total
 
-    def window_rows(mask):
-        if mask == 0:
+    def window_rows(step):
+        if step == 0:
             window_held[0] = jnp.stack(ordered(grad_out, tokens))
         else:
             places = list(window_held)
-            values = ordered(*[window_held[place] for place in places])
-            window_held.update(zip(places, values))
-        if mask + 1 < n_z:
-            hop(window_held, mask + 1)
+            window_held.update(zip(places, ordered(*[window_held[place] for place in places])))
+            chain.append(window_held[places[-1]])
+        if step < levels:
+            for mask in range(n_z):
+                if mask.bit_count() == step + 1:
+                    hop(window_held, mask)
             return
         rows_there = [window_held[mask] for k in range(2) for mask in masks[k]]
         window_held["own"] = jnp.stack(rows_there, axis=1)
@@ -525,14 +527,14 @@
             forward(1)
             send(1, 0)
         take(0, s)
+    levels = n_z.bit_length() - 1
     window_rows(0)
-    hops = iter(range(1, n_z))
+    window_rows(1)
     for s in range(1, stages - 2):
-        window_rows(next(hops))
         take(1, s - 1)
         send(1, s)
-    for mask in hops:
-        window_rows(mask)
+    for step in range(2, levels + 1):
+        window_rows(step)
     take(1, stages - 3)
     send(1, stages - 2)
     delta_terms()

time: 150 us -> 147 us (0.980)
  waiting for transfers between devices: 69.1 us -> 67.2 us
    ppermute x28, waiting for transfers between devices: 43.4 us -> 41.1 us  [over_dp(): return lax.ppermute(value, 'dp', xor_perm(n_dp, mask))]
  transfers between devices with their start and end apart: 43 -> 43, of which waited for: 23 -> 25; matrix products, arithmetic and copies ran while one was open for 3% -> 3% of each run, Pallas kernels for 14% -> 15%
where the time goes in v2:
time: 147 us
  waiting for transfers between devices  67.2 us (46%)
  starting transfers between devices  46.5 us (32%)
  Pallas kernels  25.6 us (17%)
  other arithmetic  4.23 us (3%)
  local copies, waits for them, and re-layouts  1.64 us (1%)
    ppermute x28, waiting for transfers between devices, over_dp(): return lax.ppermute(value, 'dp', xor_perm(n_dp, mask))  41.1 us
    ppermute x28, starting transfers between devices, over_dp(): return lax.ppermute(value, 'dp', xor_perm(n_dp, mask))  32.8 us
    ppermute x9, waiting for transfers between devices, over_z(): return lax.ppermute(value, 'tensor', z_perm(n_tensor, mask))  25.3 us
    ppermute x9, starting transfers between devices, over_z(): return lax.ppermute(value, 'tensor', z_perm(n_tensor, mask))  13.4 us
    pallas_call x3, Pallas kernels, forward_partials(): pl.pallas_call(functools.partial(forward_kernel, bits), out_shape=[jax.Sh...  8.8 us
    pallas_call x2, Pallas kernels, backward_partials(): pl.pallas_call(functools.partial(backward_kernel, places), out_shape=jax....  6.36 us
    pallas_call x1, Pallas kernels, window_deltas(): pl.pallas_call(functools.partial(delta_kernel, n_dp, len(hiddens)), out_s...  5.11 us
    pallas_call x1, Pallas kernels, in_vmem(): pl.pallas_call(load_kernel, out_shape=[pltpu.VMEM(w.shape, w.dtype) for w...  4.69 us
  transfers between devices with their start and end apart: 43, of which 25 were waited for; matrix products, arithmetic and copies ran while one was open for 3% of the time, Pallas kernels for 15%

profile of v2, /device:TPU:0, one launch (start us, length us, event | category | flops | bytes accessed | tf_op | source)
XLA Modules:
  0.0 146.6 jit_solution(12160646220782870181)
XLA Ops:
  1.6 3.0 %collective-permute-start = (bf16[2,16,1024]{2,1,0:T(8,128)(2,1)S(1)}, bf16[2,16,1024]{2,1,0:T(8,128)(2,1)S(1)}, u32[]{:S(2)}, u32[]{:S(2)}) collective-permute-start(bf16[2,16,1024]{2,1,0:T(8,128)(2,1)S(1)} %pad_maximum_fusion.14), channel_id=1, source_target_pairs={{0,8},{8,0},{16,24},{24,16},{1,9},{9,1},{17,25},{25,17},{2,10},{10... | collective-permute-start | bytes 196616 | tf_op jit(solution)/shard_map/ppermute | solution.py:281
  6.2 4.7 %shard_map.104 = (bf16[1024,2048]{1,0:T(8,128)(2,1)S(1)}, bf16[1024,2048]{1,0:T(8,128)(2,1)S(1)}, bf16[2048,1024]{1,0:T(8,128)(2,1)S(1)}) custom-call(bf16[1024,2048]{1,0:T(8,128)(2,1)} %refs_0_.1, bf16[1024,2048]{1,0:T(8,128)(2,1)} %refs_1_.1, bf16[2048,1024]{1,0:T(8,128)(2,1)} %refs_2_.1), custom_call_target="tpu_custom_call" | custom-call | flops 1 | bytes 1 | tf_op jit(solution)/shard_map/pallas_call | solution.py:125
  11.5 1.7 %collective-permute-start.6 = (bf16[2,4,16,1024]{3,2,1,0:T(8,128)(2,1)S(1)}, bf16[2,4,16,1024]{3,2,1,0:T(8,128)(2,1)S(1)}, u32[]{:S(2)}, u32[]{:S(2)}) collective-permute-start(bf16[2,4,16,1024]{3,2,1,0:T(8,128)(2,1)S(1)} %pad_maximum_fusion.7), channel_id=1, source_target_pairs={{0,2},{1,3},{2,0},{3,1},{4,6},{5,7},{6,4},{7,5},{8,10},{9,11},{10,... | collective-permute-start | bytes 786440 | tf_op jit(solution)/shard_map/ppermute | solution.py:287
  13.2 2.7 %shard_map.105 = (bf16[3,2,32,1024]{3,2,1,0:T(8,128)(2,1)S(1)}, bf16[3,2,32,1024]{3,2,1,0:T(8,128)(2,1)S(1)}, bf16[3,2,32,1024]{3,2,1,0:T(8,128)(2,1)S(1)}, bf16[3,2,32,1024]{3,2,1,0:T(8,128)(2,1)S(1)}) custom-call(bf16[1,2,4,16,1024]{4,3,2,1,0:T(8,128)(2,1)S(1)} %bitcast.193, bf16[1,2,4,16,1024]{4,3,2,1,0:T(8,128)(2,1)S(1)} %collective-permute-done.3.other_ref, ...), custom_call_target="tpu_custom_call" | custom-call | flops 1 | bytes 1 | tf_op jit(solution)/shard_map/pallas_call | solution.py:176
  17.5 1.6 %collective-permute-start.5 = (bf16[3,2,32,1024]{3,2,0,1:T(8,128)(2,1)S(1)}, bf16[3,2,32,1024]{3,2,0,1:T(8,128)(2,1)S(1)}, u32[]{:S(2)}, u32[]{:S(2)}) collective-permute-start(bf16[3,2,32,1024]{3,2,0,1:T(8,128)(2,1)S(1)} %copy.29), channel_id=1, source_target_pairs={{0,16},{8,24},{16,0},{24,8},{1,17},{9,25},{17,1},{25,9},{2,18},{10... | collective-permute-start | bytes 1179656 | tf_op jit(solution)/shard_map/ppermute | solution.py:281
  20.2 2.6 %collective-permute-start.10 = (bf16[2,4,16,1024]{3,2,1,0:T(8,128)(2,1)S(1)}, bf16[2,4,16,1024]{3,2,1,0:T(8,128)(2,1)S(1)}, u32[]{:S(2)}, u32[]{:S(2)}) collective-permute-start(bf16[2,4,16,1024]{3,2,1,0:T(8,128)(2,1)S(1)} %pad_maximum_fusion.7), channel_id=1, source_target_pairs={{0,4},{1,5},{2,6},{3,7},{4,0},{5,1},{6,2},{7,3},{8,12},{9,13},{10,... | collective-permute-start | bytes 786440 | tf_op jit(solution)/shard_map/ppermute | solution.py:287
  22.9 2.7 %shard_map.106 = (bf16[3,2,32,1024]{3,2,1,0:T(8,128)(2,1)S(1)}, bf16[3,2,32,1024]{3,2,1,0:T(8,128)(2,1)S(1)}, bf16[3,2,32,1024]{3,2,1,0:T(8,128)(2,1)S(1)}, bf16[3,2,32,1024]{3,2,1,0:T(8,128)(2,1)S(1)}) custom-call(bf16[1,2,4,16,1024]{4,3,2,1,0:T(8,128)(2,1)S(1)} %bitcast.195, bf16[1,2,4,16,1024]{4,3,2,1,0:T(8,128)(2,1)S(1)} %collective-permute-done.7.other_ref, ...), custom_call_target="tpu_custom_call" | custom-call | flops 1 | bytes 1 | tf_op jit(solution)/shard_map/pallas_call | solution.py:176
  27.2 1.6 %collective-permute-start.9 = (bf16[3,2,32,1024]{3,2,0,1:T(8,128)(2,1)S(1)}, bf16[3,2,32,1024]{3,2,0,1:T(8,128)(2,1)S(1)}, u32[]{:S(2)}, u32[]{:S(2)}) collective-permute-start(bf16[3,2,32,1024]{3,2,0,1:T(8,128)(2,1)S(1)} %copy.32), channel_id=1, source_target_pairs={{0,16},{8,24},{16,0},{24,8},{1,17},{9,25},{17,1},{25,9},{2,18},{10... | collective-permute-start | bytes 1179656 | tf_op jit(solution)/shard_map/ppermute | solution.py:281
  29.0 6.5 %collective-permute-done.10 = bf16[2,4,16,1024]{3,2,1,0:T(8,128)(2,1)S(1)} collective-permute-done((bf16[2,4,16,1024]{3,2,1,0:T(8,128)(2,1)S(1)}, bf16[2,4,16,1024]{3,2,1,0:T(8,128)(2,1)S(1)}, u32[]{:S(2)}, u32[]{:S(2)}) %collective-permute-start.10) | collective-permute-done | bytes 262176 | tf_op jit(solution)/shard_map/ppermute | solution.py:287
  42.7 6.4 %collective-permute-done.11 = bf16[3,64,1024]{2,1,0:T(8,128)(2,1)S(1)} collective-permute-done((bf16[3,64,1024]{2,1,0:T(8,128)(2,1)S(1)}, bf16[3,64,1024]{2,1,0:T(8,128)(2,1)S(1)}, u32[]{:S(2)}, u32[]{:S(2)}) %collective-permute-start.11) | collective-permute-done | bytes 393248 | tf_op jit(solution)/shard_map/ppermute | solution.py:281
  53.2 3.5 %shard_map.107 = (bf16[3,2,64,1024]{3,2,1,0:T(8,128)(2,1)S(1)}, bf16[3,2,64,1024]{3,2,1,0:T(8,128)(2,1)S(1)}, bf16[3,2,64,1024]{3,2,1,0:T(8,128)(2,1)S(1)}, bf16[3,2,64,1024]{3,2,1,0:T(8,128)(2,1)S(1)}) custom-call(bf16[2,2,4,16,1024]{4,3,2,1,0:T(8,128)(2,1)S(1)} %pad_maximum_fusion.5.own_ref, ...), custom_call_target="tpu_custom_call" | custom-call | flops 1 | bytes 1 | tf_op jit(solution)/shard_map/pallas_call | solution.py:176
  61.0 1.6 %collective-permute-start.17 = (bf16[2,16,4096]{2,1,0:T(8,128)(2,1)S(1)}, bf16[2,16,4096]{2,1,0:T(8,128)(2,1)S(1)}, u32[]{:S(2)}, u32[]{:S(2)}) collective-permute-start(bf16[2,16,4096]{2,1,0:T(8,128)(2,1)S(1)} %pad_maximum_fusion.10), channel_id=1, source_target_pairs={{0,2},{1,3},{2,0},{3,1},{4,6},{5,7},{6,4},{7,5},{8,10},{9,11},{10,... | collective-permute-start | bytes 786440 | tf_op jit(solution)/shard_map/ppermute | solution.py:287
  63.9 8.4 %collective-permute-done.17 = bf16[2,16,4096]{2,1,0:T(8,128)(2,1)S(1)} collective-permute-done((bf16[2,16,4096]{2,1,0:T(8,128)(2,1)S(1)}, bf16[2,16,4096]{2,1,0:T(8,128)(2,1)S(1)}, u32[]{:S(2)}, u32[]{:S(2)}) %collective-permute-start.17) | collective-permute-done | bytes 262176 | tf_op jit(solution)/shard_map/ppermute | solution.py:287
  72.3 3.7 %collective-permute-done.18 = bf16[2,16,4096]{2,1,0:T(8,128)(2,1)S(1)} collective-permute-done((bf16[2,16,4096]{2,1,0:T(8,128)(2,1)S(1)}, bf16[2,16,4096]{2,1,0:T(8,128)(2,1)S(1)}, u32[]{:S(2)}, u32[]{:S(2)}) %collective-permute-start.18) | collective-permute-done | bytes 262176 | tf_op jit(solution)/shard_map/ppermute | solution.py:287
  80.0 2.4 %collective-permute-done.19 = bf16[2,16,4096]{2,1,0:T(8,128)(2,1)S(1)} collective-permute-done((bf16[2,16,4096]{2,1,0:T(8,128)(2,1)S(1)}, bf16[2,16,4096]{2,1,0:T(8,128)(2,1)S(1)}, u32[]{:S(2)}, u32[]{:S(2)}) %collective-permute-start.19) | collective-permute-done | bytes 262176 | tf_op jit(solution)/shard_map/ppermute | solution.py:287
  82.6 5.7 %collective-permute-done.23 = bf16[3,64,1024]{2,1,0:T(8,128)(2,1)S(1)} collective-permute-done((bf16[3,64,1024]{2,1,0:T(8,128)(2,1)S(1)}, bf16[3,64,1024]{2,1,0:T(8,128)(2,1)S(1)}, u32[]{:S(2)}, u32[]{:S(2)}) %collective-permute-start.23) | collective-permute-done | bytes 393248 | tf_op jit(solution)/shard_map/ppermute | solution.py:281
  91.9 5.1 %shard_map.108 = f32[20,128,128]{2,1,0:T(8,128)S(1)} custom-call(s32[1]{0:T(128)} %bitcast.me_ref, s32[20]{0:T(128)S(1)} %copy-done, s32[20]{0:T(128)S(1)} %copy-done.1, s32[20]{0:T(128)S(1)} %copy-done.2, s32[20]{0:T(128)S(1)} %bitcast.196, bf16[2,4,16,4096]{3,2,1,0:T(8,128)(2,1)S(1)} %pad_maximum_fusion.2.refs_0_, ...), custom_call_target="tpu_custom_call" | custom-call | flops 1 | bytes 1 | tf_op jit(solution)/shard_map/pallas_call | solution.py:94
  102.0 15.8 %collective-permute-done.25 = bf16[2,5,64,128]{3,2,1,0:T(8,128)(2,1)S(1)} collective-permute-done((bf16[2,5,64,128]{3,2,1,0:T(8,128)(2,1)S(1)}, bf16[2,5,64,128]{3,2,1,0:T(8,128)(2,1)S(1)}, u32[]{:S(2)}, u32[]{:S(2)}) %collective-permute-start.25) | collective-permute-done | bytes 163872 | tf_op jit(solution)/shard_map/ppermute | solution.py:281
  119.0 3.5 %shard_map.109 = f32[384,1024]{1,0:T(8,128)S(1)} custom-call(bf16[2,2,96,1024]{3,2,1,0:T(8,128)(2,1)S(1)} %maximum_maximum_fusion.refs_0_, bf16[2,2,96,1024]{3,2,1,0:T(8,128)(2,1)S(1)} %collective-permute-done.31.refs_1_, bf16[2,2,96,1024]{3,2,1,0:T(8,128)(2,1)S(1)} %maximum_maximum_fusion.1.refs_2_, ...), custom_call_target="tpu_custom_call" | custom-call | flops 1 | bytes 1 | tf_op jit(solution)/shard_map/pallas_call | solution.py:214
  124.7 1.6 %collective-permute-start.34 = (bf16[4,16,1024]{2,1,0:T(8,128)(2,1)S(1)}, bf16[4,16,1024]{2,1,0:T(8,128)(2,1)S(1)}, u32[]{:S(2)}, u32[]{:S(2)}) collective-permute-start(bf16[4,16,1024]{2,1,0:T(8,128)(2,1)S(1)} %get-tuple-element.202), channel_id=1, source_target_pairs={{0,2},{1,3},{2,0},{3,1},{4,6},{5,7},{6,4},{7,5},{8,10},{9,11},{10,... | collective-permute-start | bytes 393224 | tf_op jit(solution)/shard_map/ppermute | solution.py:287
  126.3 1.7 %collective-permute-start.36 = (bf16[4,16,1024]{2,1,0:T(8,128)(2,1)S(1)}, bf16[4,16,1024]{2,1,0:T(8,128)(2,1)S(1)}, u32[]{:S(2)}, u32[]{:S(2)}) collective-permute-start(bf16[4,16,1024]{2,1,0:T(8,128)(2,1)S(1)} %get-tuple-element.203), channel_id=1, source_target_pairs={{0,4},{1,5},{2,6},{3,7},{4,0},{5,1},{6,2},{7,3},{8,12},{9,13},{10,... | collective-permute-start | bytes 393224 | tf_op jit(solution)/shard_map/ppermute | solution.py:287
  129.1 2.0 %collective-permute-done.34 = bf16[4,16,1024]{2,1,0:T(8,128)(2,1)S(1)} collective-permute-done((bf16[4,16,1024]{2,1,0:T(8,128)(2,1)S(1)}, bf16[4,16,1024]{2,1,0:T(8,128)(2,1)S(1)}, u32[]{:S(2)}, u32[]{:S(2)}) %collective-permute-start.34) | collective-permute-done | bytes 131104 | tf_op jit(solution)/shard_map/ppermute | solution.py:287
  131.6 2.9 %shard_map.110 = f32[128,1024]{1,0:T(8,128)S(1)} custom-call(bf16[2,2,32,1024]{3,2,1,0:T(8,128)(2,1)S(1)} %get-tuple-element.168.refs_0_, bf16[2,2,32,1024]{3,2,1,0:T(8,128)(2,1)S(1)} %collective-permute-done.29.refs_1_, bf16[2,2,32,1024]{3,2,1,0:T(8,128)(2,1)S(1)} %get-tuple-element.169.refs_2_, ...), custom_call_target="tpu_custom_call" | custom-call | flops 1 | bytes 1 | tf_op jit(solution)/shard_map/pallas_call | solution.py:214
  144.3 1.7 %collective-permute-done.40.refs_3_ = bf16[16,1024]{1,0:T(8,128)(2,1)S(1)} collective-permute-done((bf16[16,1024]{1,0:T(8,128)(2,1)S(1)}, bf16[16,1024]{1,0:T(8,128)(2,1)S(1)}, u32[]{:S(2)}, u32[]{:S(2)}) %collective-permute-start.40) | collective-permute-done | bytes 32800 | tf_op jit(solution)/shard_map/ppermute | solution.py:281
  (147 shorter events, 52.3 us)
Async XLA Ops:
  1.6 9.4 %collective-permute-start = (bf16[2,16,1024]{2,1,0:T(8,128)(2,1)S(1)}, bf16[2,16,1024]{2,1,0:T(8,128)(2,1)S(1)}, u32[]{:S(2)}, u32[]{:S(2)}) collective-permute-start(bf16[2,16,1024]{2,1,0:T(8,128)(2,1)S(1)} %pad_maximum_fusion.14), channel_id=1, source_target_pairs={{0,8},{8,0},{16,24},{24,16},{1,9},{9,1},{17,25},{25,17},{2,10},{10... | collective-permute-start | bytes 196616 | tf_op jit(solution)/shard_map/ppermute | solution.py:281
  15.9 12.9 %collective-permute-start.4 = (bf16[3,2,32,1024]{3,2,0,1:T(8,128)(2,1)S(1)}, bf16[3,2,32,1024]{3,2,0,1:T(8,128)(2,1)S(1)}, u32[]{:S(2)}, u32[]{:S(2)}) collective-permute-start(bf16[3,2,32,1024]{3,2,0,1:T(8,128)(2,1)S(1)} %copy.28), channel_id=1, source_target_pairs={{0,8},{8,0},{16,24},{24,16},{1,9},{9,1},{17,25},{25,17},{2,10},{10... | collective-permute-start | bytes 1179656 | tf_op jit(solution)/shard_map/ppermute | solution.py:281
  17.5 11.3 %collective-permute-start.5 = (bf16[3,2,32,1024]{3,2,0,1:T(8,128)(2,1)S(1)}, bf16[3,2,32,1024]{3,2,0,1:T(8,128)(2,1)S(1)}, u32[]{:S(2)}, u32[]{:S(2)}) collective-permute-start(bf16[3,2,32,1024]{3,2,0,1:T(8,128)(2,1)S(1)} %copy.29), channel_id=1, source_target_pairs={{0,16},{8,24},{16,0},{24,8},{1,17},{9,25},{17,1},{25,9},{2,18},{10... | collective-permute-start | bytes 1179656 | tf_op jit(solution)/shard_map/ppermute | solution.py:281
  20.2 15.2 %collective-permute-start.10 = (bf16[2,4,16,1024]{3,2,1,0:T(8,128)(2,1)S(1)}, bf16[2,4,16,1024]{3,2,1,0:T(8,128)(2,1)S(1)}, u32[]{:S(2)}, u32[]{:S(2)}) collective-permute-start(bf16[2,4,16,1024]{3,2,1,0:T(8,128)(2,1)S(1)} %pad_maximum_fusion.7), channel_id=1, source_target_pairs={{0,4},{1,5},{2,6},{3,7},{4,0},{5,1},{6,2},{7,3},{8,12},{9,13},{10,... | collective-permute-start | bytes 786440 | tf_op jit(solution)/shard_map/ppermute | solution.py:287
  25.6 11.3 %collective-permute-start.8 = (bf16[3,2,32,1024]{3,2,0,1:T(8,128)(2,1)S(1)}, bf16[3,2,32,1024]{3,2,0,1:T(8,128)(2,1)S(1)}, u32[]{:S(2)}, u32[]{:S(2)}) collective-permute-start(bf16[3,2,32,1024]{3,2,0,1:T(8,128)(2,1)S(1)} %copy.31), channel_id=1, source_target_pairs={{0,8},{8,0},{16,24},{24,16},{1,9},{9,1},{17,25},{25,17},{2,10},{10... | collective-permute-start | bytes 1179656 | tf_op jit(solution)/shard_map/ppermute | solution.py:281
  27.2 11.0 %collective-permute-start.9 = (bf16[3,2,32,1024]{3,2,0,1:T(8,128)(2,1)S(1)}, bf16[3,2,32,1024]{3,2,0,1:T(8,128)(2,1)S(1)}, u32[]{:S(2)}, u32[]{:S(2)}) collective-permute-start(bf16[3,2,32,1024]{3,2,0,1:T(8,128)(2,1)S(1)} %copy.32), channel_id=1, source_target_pairs={{0,16},{8,24},{16,0},{24,8},{1,17},{9,25},{17,1},{25,9},{2,18},{10... | collective-permute-start | bytes 1179656 | tf_op jit(solution)/shard_map/ppermute | solution.py:281
  38.9 10.2 %collective-permute-start.11 = (bf16[3,64,1024]{2,1,0:T(8,128)(2,1)S(1)}, bf16[3,64,1024]{2,1,0:T(8,128)(2,1)S(1)}, u32[]{:S(2)}, u32[]{:S(2)}) collective-permute-start(bf16[3,64,1024]{2,1,0:T(8,128)(2,1)S(1)} %fusion.2), channel_id=1, source_target_pairs={{0,16},{8,24},{16,0},{24,8},{1,17},{9,25},{17,1},{25,9},{2,18},{10... | collective-permute-start | bytes 1179656 | tf_op jit(solution)/shard_map/ppermute | solution.py:281
  40.5 9.9 %collective-permute-start.12 = (bf16[3,64,1024]{2,1,0:T(8,128)(2,1)S(1)}, bf16[3,64,1024]{2,1,0:T(8,128)(2,1)S(1)}, u32[]{:S(2)}, u32[]{:S(2)}) collective-permute-start(bf16[3,64,1024]{2,1,0:T(8,128)(2,1)S(1)} %fusion.3), channel_id=1, source_target_pairs={{0,8},{8,0},{16,24},{24,16},{1,9},{9,1},{17,25},{25,17},{2,10},{10... | collective-permute-start | bytes 1179656 | tf_op jit(solution)/shard_map/ppermute | solution.py:281
  41.1 10.0 %collective-permute-start.15 = (bf16[2,4,16,1024]{3,2,1,0:T(8,128)(2,1)S(1)}, bf16[2,4,16,1024]{3,2,1,0:T(8,128)(2,1)S(1)}, u32[]{:S(2)}, u32[]{:S(2)}) collective-permute-start(bf16[2,4,16,1024]{3,2,1,0:T(8,128)(2,1)S(1)} %collective-permute-done.10), channel_id=1, source_target_pairs={{0,2},{1,3},{2,0},{3,1},{4,6},{5,7},{6,4},{7,5},{8,10},{9,11},{10,... | collective-permute-start | bytes 786440 | tf_op jit(solution)/shard_map/ppermute | solution.py:287
  51.3 8.7 %collective-permute-start.13 = (bf16[2,64,1024]{2,1,0:T(8,128)(2,1)S(1)}, bf16[2,64,1024]{2,1,0:T(8,128)(2,1)S(1)}, u32[]{:S(2)}, u32[]{:S(2)}) collective-permute-start(bf16[2,64,1024]{2,1,0:T(8,128)(2,1)S(1)} %pad_maximum_fusion.8.refs_6_), channel_id=1, source_target_pairs={{0,16},{8,24},{16,0},{24,8},{1,17},{9,25},{17,1},{25,9},{2,18},{10... | collective-permute-start | bytes 786440 | tf_op jit(solution)/shard_map/ppermute | solution.py:281
  51.9 9.0 %collective-permute-start.14 = (bf16[2,64,1024]{2,1,0:T(8,128)(2,1)S(1)}, bf16[2,64,1024]{2,1,0:T(8,128)(2,1)S(1)}, u32[]{:S(2)}, u32[]{:S(2)}) collective-permute-start(bf16[2,64,1024]{2,1,0:T(8,128)(2,1)S(1)} %pad_maximum_fusion.9.refs_7_), channel_id=1, source_target_pairs={{0,8},{8,0},{16,24},{24,16},{1,9},{9,1},{17,25},{25,17},{2,10},{10... | collective-permute-start | bytes 786440 | tf_op jit(solution)/shard_map/ppermute | solution.py:281
  56.7 20.4 %collective-permute-start.20 = (bf16[3,2,64,1024]{3,2,0,1:T(8,128)(2,1)S(1)}, bf16[3,2,64,1024]{3,2,0,1:T(8,128)(2,1)S(1)}, u32[]{:S(2)}, u32[]{:S(2)}) collective-permute-start(bf16[3,2,64,1024]{3,2,0,1:T(8,128)(2,1)S(1)} %copy.36), channel_id=1, source_target_pairs={{0,8},{8,0},{16,24},{24,16},{1,9},{9,1},{17,25},{25,17},{2,10},{10... | collective-permute-start | bytes 2359304 | tf_op jit(solution)/shard_map/ppermute | solution.py:281
  57.6 19.5 %collective-permute-start.21 = (bf16[3,2,64,1024]{3,2,0,1:T(8,128)(2,1)S(1)}, bf16[3,2,64,1024]{3,2,0,1:T(8,128)(2,1)S(1)}, u32[]{:S(2)}, u32[]{:S(2)}) collective-permute-start(bf16[3,2,64,1024]{3,2,0,1:T(8,128)(2,1)S(1)} %copy.37), channel_id=1, source_target_pairs={{0,16},{8,24},{16,0},{24,8},{1,17},{9,25},{17,1},{25,9},{2,18},{10... | collective-permute-start | bytes 2359304 | tf_op jit(solution)/shard_map/ppermute | solution.py:281
  61.0 11.3 %collective-permute-start.17 = (bf16[2,16,4096]{2,1,0:T(8,128)(2,1)S(1)}, bf16[2,16,4096]{2,1,0:T(8,128)(2,1)S(1)}, u32[]{:S(2)}, u32[]{:S(2)}) collective-permute-start(bf16[2,16,4096]{2,1,0:T(8,128)(2,1)S(1)} %pad_maximum_fusion.10), channel_id=1, source_target_pairs={{0,2},{1,3},{2,0},{3,1},{4,6},{5,7},{6,4},{7,5},{8,10},{9,11},{10,... | collective-permute-start | bytes 786440 | tf_op jit(solution)/shard_map/ppermute | solution.py:287
  62.6 13.4 %collective-permute-start.18 = (bf16[2,16,4096]{2,1,0:T(8,128)(2,1)S(1)}, bf16[2,16,4096]{2,1,0:T(8,128)(2,1)S(1)}, u32[]{:S(2)}, u32[]{:S(2)}) collective-permute-start(bf16[2,16,4096]{2,1,0:T(8,128)(2,1)S(1)} %pad_maximum_fusion.10), channel_id=1, source_target_pairs={{0,4},{1,5},{2,6},{3,7},{4,0},{5,1},{6,2},{7,3},{8,12},{9,13},{10,... | collective-permute-start | bytes 786440 | tf_op jit(solution)/shard_map/ppermute | solution.py:287
  77.8 10.5 %collective-permute-start.23 = (bf16[3,64,1024]{2,1,0:T(8,128)(2,1)S(1)}, bf16[3,64,1024]{2,1,0:T(8,128)(2,1)S(1)}, u32[]{:S(2)}, u32[]{:S(2)}) collective-permute-start(bf16[3,64,1024]{2,1,0:T(8,128)(2,1)S(1)} %fusion.4), channel_id=1, source_target_pairs={{0,16},{8,24},{16,0},{24,8},{1,17},{9,25},{17,1},{25,9},{2,18},{10... | collective-permute-start | bytes 1179656 | tf_op jit(solution)/shard_map/ppermute | solution.py:281
  79.4 10.1 %collective-permute-start.24 = (bf16[3,64,1024]{2,1,0:T(8,128)(2,1)S(1)}, bf16[3,64,1024]{2,1,0:T(8,128)(2,1)S(1)}, u32[]{:S(2)}, u32[]{:S(2)}) collective-permute-start(bf16[3,64,1024]{2,1,0:T(8,128)(2,1)S(1)} %fusion.5), channel_id=1, source_target_pairs={{0,8},{8,0},{16,24},{24,16},{1,9},{9,1},{17,25},{25,17},{2,10},{10... | collective-permute-start | bytes 1179656 | tf_op jit(solution)/shard_map/ppermute | solution.py:281
  82.5 9.3 %collective-permute-start.22 = (bf16[2,4,16,4096]{3,2,1,0:T(8,128)(2,1)S(1)}, bf16[2,4,16,4096]{3,2,1,0:T(8,128)(2,1)S(1)}, u32[]{:S(2)}, u32[]{:S(2)}) collective-permute-start(bf16[2,4,16,4096]{3,2,1,0:T(8,128)(2,1)S(1)} %pad_maximum_fusion.2.refs_0_), channel_id=1, source_target_pairs={{0,1},{1,0},{2,3},{3,2},{4,5},{5,4},{6,7},{7,6},{8,9},{9,8},{10,11... | collective-permute-start | bytes 3145736 | tf_op jit(solution)/shard_map/ppermute | solution.py:284
  97.6 21.4 %collective-permute-start.31 = (bf16[2,2,96,1024]{3,2,1,0:T(8,128)(2,1)S(1)}, bf16[2,2,96,1024]{3,2,1,0:T(8,128)(2,1)S(1)}, u32[]{:S(2)}, u32[]{:S(2)}) collective-permute-start(bf16[2,2,96,1024]{3,2,1,0:T(8,128)(2,1)S(1)} %maximum_maximum_fusion.refs_0_), channel_id=1, source_target_pairs={{0,8},{8,0},{16,24},{24,16},{1,9},{9,1},{17,25},{25,17},{2,10},{10... | collective-permute-start | bytes 2359304 | tf_op jit(solution)/shard_map/ppermute | solution.py:281
  98.5 20.5 %collective-permute-start.32 = (bf16[2,2,96,1024]{3,2,1,0:T(8,128)(2,1)S(1)}, bf16[2,2,96,1024]{3,2,1,0:T(8,128)(2,1)S(1)}, u32[]{:S(2)}, u32[]{:S(2)}) collective-permute-start(bf16[2,2,96,1024]{3,2,1,0:T(8,128)(2,1)S(1)} %maximum_maximum_fusion.1.refs_2_), channel_id=1, source_target_pairs={{0,16},{8,24},{16,0},{24,8},{1,17},{9,25},{17,1},{25,9},{2,18},{10... | collective-permute-start | bytes 2359304 | tf_op jit(solution)/shard_map/ppermute | solution.py:281
  100.1 17.7 %collective-permute-start.25 = (bf16[2,5,64,128]{3,2,1,0:T(8,128)(2,1)S(1)}, bf16[2,5,64,128]{3,2,1,0:T(8,128)(2,1)S(1)}, u32[]{:S(2)}, u32[]{:S(2)}) collective-permute-start(bf16[2,5,64,128]{3,2,1,0:T(8,128)(2,1)S(1)} %fusion.30), channel_id=1, source_target_pairs={{0,8},{8,0},{16,24},{24,16},{1,9},{9,1},{17,25},{25,17},{2,10},{10... | collective-permute-start | bytes 491528 | tf_op jit(solution)/shard_map/ppermute | solution.py:281
  101.3 17.6 %collective-permute-start.26 = (bf16[2,5,64,128]{3,2,1,0:T(8,128)(2,1)S(1)}, bf16[2,5,64,128]{3,2,1,0:T(8,128)(2,1)S(1)}, u32[]{:S(2)}, u32[]{:S(2)}) collective-permute-start(bf16[2,5,64,128]{3,2,1,0:T(8,128)(2,1)S(1)} %fusion.31), channel_id=1, source_target_pairs={{0,16},{8,24},{16,0},{24,8},{1,17},{9,25},{17,1},{25,9},{2,18},{10... | collective-permute-start | bytes 491528 | tf_op jit(solution)/shard_map/ppermute | solution.py:281
  126.3 12.5 %collective-permute-start.36 = (bf16[4,16,1024]{2,1,0:T(8,128)(2,1)S(1)}, bf16[4,16,1024]{2,1,0:T(8,128)(2,1)S(1)}, u32[]{:S(2)}, u32[]{:S(2)}) collective-permute-start(bf16[4,16,1024]{2,1,0:T(8,128)(2,1)S(1)} %get-tuple-element.203), channel_id=1, source_target_pairs={{0,4},{1,5},{2,6},{3,7},{4,0},{5,1},{6,2},{7,3},{8,12},{9,13},{10,... | collective-permute-start | bytes 393224 | tf_op jit(solution)/shard_map/ppermute | solution.py:287
  128.0 10.8 %collective-permute-start.37 = (bf16[4,16,1024]{2,1,0:T(8,128)(2,1)S(1)}, bf16[4,16,1024]{2,1,0:T(8,128)(2,1)S(1)}, u32[]{:S(2)}, u32[]{:S(2)}) collective-permute-start(bf16[4,16,1024]{2,1,0:T(8,128)(2,1)S(1)} %get-tuple-element.204), channel_id=1, source_target_pairs={{0,6},{1,7},{2,4},{3,5},{4,2},{5,3},{6,0},{7,1},{8,14},{9,15},{10,... | collective-permute-start | bytes 393224 | tf_op jit(solution)/shard_map/ppermute | solution.py:287
  (25 other events, 117.8 us)

commit v3 on v2

--- a/solution.py
+++ b/solution.py
@@ -111,10 +111,12 @@
 
 def load_kernel(*refs):
     n = (len(refs) - 1) // 2
-    copies = [
-        pltpu.make_async_copy(source, target, refs[-1].at[i])
-        for i, (source, target) in enumerate(zip(refs[:n], refs[n : 2 * n]))
-    ]
+    copies = []
+    for i, (source, target) in enumerate(zip(refs[:n], refs[n : 2 * n])):
+        rows = source.shape[0] // 4
+        for j in range(4):
+            cut = pl.ds(j * rows, rows)
+            copies.append(pltpu.make_async_copy(source.at[cut], target.at[cut], refs[-1].at[i, j]))
     for copy in copies:
         copy.start()
     for copy in copies:
@@ -127,7 +129,7 @@
         out_shape=[pltpu.VMEM(w.shape, w.dtype) for w in weights],
         in_specs=[pl.BlockSpec(memory_space=pl.ANY)] * len(weights),
         out_specs=[pl.BlockSpec(memory_space=pltpu.VMEM)] * len(weights),
-        scratch_shapes=[pltpu.SemaphoreType.DMA((len(weights),))],
+        scratch_shapes=[pltpu.SemaphoreType.DMA((len(weights), 4))],
         compiler_params=pltpu.CompilerParams(vmem_limit_bytes=1 << 20),
         cost_estimate=SMALL,
     )(*[pltpu.with_memory_space_constraint(w, pltpu.HBM) for w in weights])

time: 147 us -> 147 us (level)
  no operation moved by 1% of the time
where the time goes in v3:
time: 147 us
  waiting for transfers between devices  67.3 us (46%)
  starting transfers between devices  46.5 us (32%)
  Pallas kernels  25.6 us (17%)
  other arithmetic  4.23 us (3%)
  local copies, waits for them, and re-layouts  1.64 us (1%)
    ppermute x28, waiting for transfers between devices, over_dp(): return lax.ppermute(value, 'dp', xor_perm(n_dp, mask))  40.9 us
    ppermute x28, starting transfers between devices, over_dp(): return lax.ppermute(value, 'dp', xor_perm(n_dp, mask))  32.7 us
    ppermute x9, waiting for transfers between devices, over_z(): return lax.ppermute(value, 'tensor', z_perm(n_tensor, mask))  25.6 us
    ppermute x9, starting transfers between devices, over_z(): return lax.ppermute(value, 'tensor', z_perm(n_tensor, mask))  13.4 us
    pallas_call x3, Pallas kernels, forward_partials(): pl.pallas_call(functools.partial(forward_kernel, bits), out_shape=[jax.Sh...  8.8 us
    pallas_call x2, Pallas kernels, backward_partials(): pl.pallas_call(functools.partial(backward_kernel, places), out_shape=jax....  6.36 us
    pallas_call x1, Pallas kernels, window_deltas(): pl.pallas_call(functools.partial(delta_kernel, n_dp, len(hiddens)), out_s...  5.11 us
    pallas_call x1, Pallas kernels, in_vmem(): pl.pallas_call(load_kernel, out_shape=[pltpu.VMEM(w.shape, w.dtype) for w...  4.71 us
  transfers between devices with their start and end apart: 43, of which 25 were waited for; matrix products, arithmetic and copies ran while one was open for 3% of the time, Pallas kernels for 15%

profile of v3, /device:TPU:0, one launch (start us, length us, event | category | flops | bytes accessed | tf_op | source)
XLA Modules:
  0.0 146.6 jit_solution(5411347871685309405)
XLA Ops:
  1.6 3.0 %collective-permute-start = (bf16[2,16,1024]{2,1,0:T(8,128)(2,1)S(1)}, bf16[2,16,1024]{2,1,0:T(8,128)(2,1)S(1)}, u32[]{:S(2)}, u32[]{:S(2)}) collective-permute-start(bf16[2,16,1024]{2,1,0:T(8,128)(2,1)S(1)} %pad_maximum_fusion.14), channel_id=1, source_target_pairs={{0,8},{8,0},{16,24},{24,16},{1,9},{9,1},{17,25},{25,17},{2,10},{10... | collective-permute-start | bytes 196616 | tf_op jit(solution)/shard_map/ppermute | solution.py:283
  6.2 4.7 %shard_map.104 = (bf16[1024,2048]{1,0:T(8,128)(2,1)S(1)}, bf16[1024,2048]{1,0:T(8,128)(2,1)S(1)}, bf16[2048,1024]{1,0:T(8,128)(2,1)S(1)}) custom-call(bf16[1024,2048]{1,0:T(8,128)(2,1)} %refs_0_.1, bf16[1024,2048]{1,0:T(8,128)(2,1)} %refs_1_.1, bf16[2048,1024]{1,0:T(8,128)(2,1)} %refs_2_.1), custom_call_target="tpu_custom_call" | custom-call | flops 1 | bytes 1 | tf_op jit(solution)/shard_map/pallas_call | solution.py:127
  11.5 1.7 %collective-permute-start.6 = (bf16[2,4,16,1024]{3,2,1,0:T(8,128)(2,1)S(1)}, bf16[2,4,16,1024]{3,2,1,0:T(8,128)(2,1)S(1)}, u32[]{:S(2)}, u32[]{:S(2)}) collective-permute-start(bf16[2,4,16,1024]{3,2,1,0:T(8,128)(2,1)S(1)} %pad_maximum_fusion.7), channel_id=1, source_target_pairs={{0,2},{1,3},{2,0},{3,1},{4,6},{5,7},{6,4},{7,5},{8,10},{9,11},{10,... | collective-permute-start | bytes 786440 | tf_op jit(solution)/shard_map/ppermute | solution.py:289
  13.2 2.7 %shard_map.105 = (bf16[3,2,32,1024]{3,2,1,0:T(8,128)(2,1)S(1)}, bf16[3,2,32,1024]{3,2,1,0:T(8,128)(2,1)S(1)}, bf16[3,2,32,1024]{3,2,1,0:T(8,128)(2,1)S(1)}, bf16[3,2,32,1024]{3,2,1,0:T(8,128)(2,1)S(1)}) custom-call(bf16[1,2,4,16,1024]{4,3,2,1,0:T(8,128)(2,1)S(1)} %bitcast.193, bf16[1,2,4,16,1024]{4,3,2,1,0:T(8,128)(2,1)S(1)} %collective-permute-done.3.other_ref, ...), custom_call_target="tpu_custom_call" | custom-call | flops 1 | bytes 1 | tf_op jit(solution)/shard_map/pallas_call | solution.py:178
  17.6 1.6 %collective-permute-start.5 = (bf16[3,2,32,1024]{3,2,0,1:T(8,128)(2,1)S(1)}, bf16[3,2,32,1024]{3,2,0,1:T(8,128)(2,1)S(1)}, u32[]{:S(2)}, u32[]{:S(2)}) collective-permute-start(bf16[3,2,32,1024]{3,2,0,1:T(8,128)(2,1)S(1)} %copy.29), channel_id=1, source_target_pairs={{0,16},{8,24},{16,0},{24,8},{1,17},{9,25},{17,1},{25,9},{2,18},{10... | collective-permute-start | bytes 1179656 | tf_op jit(solution)/shard_map/ppermute | solution.py:283
  20.2 2.7 %collective-permute-start.10 = (bf16[2,4,16,1024]{3,2,1,0:T(8,128)(2,1)S(1)}, bf16[2,4,16,1024]{3,2,1,0:T(8,128)(2,1)S(1)}, u32[]{:S(2)}, u32[]{:S(2)}) collective-permute-start(bf16[2,4,16,1024]{3,2,1,0:T(8,128)(2,1)S(1)} %pad_maximum_fusion.7), channel_id=1, source_target_pairs={{0,4},{1,5},{2,6},{3,7},{4,0},{5,1},{6,2},{7,3},{8,12},{9,13},{10,... | collective-permute-start | bytes 786440 | tf_op jit(solution)/shard_map/ppermute | solution.py:289
  22.9 2.7 %shard_map.106 = (bf16[3,2,32,1024]{3,2,1,0:T(8,128)(2,1)S(1)}, bf16[3,2,32,1024]{3,2,1,0:T(8,128)(2,1)S(1)}, bf16[3,2,32,1024]{3,2,1,0:T(8,128)(2,1)S(1)}, bf16[3,2,32,1024]{3,2,1,0:T(8,128)(2,1)S(1)}) custom-call(bf16[1,2,4,16,1024]{4,3,2,1,0:T(8,128)(2,1)S(1)} %bitcast.195, bf16[1,2,4,16,1024]{4,3,2,1,0:T(8,128)(2,1)S(1)} %collective-permute-done.7.other_ref, ...), custom_call_target="tpu_custom_call" | custom-call | flops 1 | bytes 1 | tf_op jit(solution)/shard_map/pallas_call | solution.py:178
  27.2 1.6 %collective-permute-start.9 = (bf16[3,2,32,1024]{3,2,0,1:T(8,128)(2,1)S(1)}, bf16[3,2,32,1024]{3,2,0,1:T(8,128)(2,1)S(1)}, u32[]{:S(2)}, u32[]{:S(2)}) collective-permute-start(bf16[3,2,32,1024]{3,2,0,1:T(8,128)(2,1)S(1)} %copy.32), channel_id=1, source_target_pairs={{0,16},{8,24},{16,0},{24,8},{1,17},{9,25},{17,1},{25,9},{2,18},{10... | collective-permute-start | bytes 1179656 | tf_op jit(solution)/shard_map/ppermute | solution.py:283
  29.0 6.5 %collective-permute-done.10 = bf16[2,4,16,1024]{3,2,1,0:T(8,128)(2,1)S(1)} collective-permute-done((bf16[2,4,16,1024]{3,2,1,0:T(8,128)(2,1)S(1)}, bf16[2,4,16,1024]{3,2,1,0:T(8,128)(2,1)S(1)}, u32[]{:S(2)}, u32[]{:S(2)}) %collective-permute-start.10) | collective-permute-done | bytes 262176 | tf_op jit(solution)/shard_map/ppermute | solution.py:289
  42.7 6.4 %collective-permute-done.11 = bf16[3,64,1024]{2,1,0:T(8,128)(2,1)S(1)} collective-permute-done((bf16[3,64,1024]{2,1,0:T(8,128)(2,1)S(1)}, bf16[3,64,1024]{2,1,0:T(8,128)(2,1)S(1)}, u32[]{:S(2)}, u32[]{:S(2)}) %collective-permute-start.11) | collective-permute-done | bytes 393248 | tf_op jit(solution)/shard_map/ppermute | solution.py:283
  53.2 3.5 %shard_map.107 = (bf16[3,2,64,1024]{3,2,1,0:T(8,128)(2,1)S(1)}, bf16[3,2,64,1024]{3,2,1,0:T(8,128)(2,1)S(1)}, bf16[3,2,64,1024]{3,2,1,0:T(8,128)(2,1)S(1)}, bf16[3,2,64,1024]{3,2,1,0:T(8,128)(2,1)S(1)}) custom-call(bf16[2,2,4,16,1024]{4,3,2,1,0:T(8,128)(2,1)S(1)} %pad_maximum_fusion.5.own_ref, ...), custom_call_target="tpu_custom_call" | custom-call | flops 1 | bytes 1 | tf_op jit(solution)/shard_map/pallas_call | solution.py:178
  61.0 1.6 %collective-permute-start.17 = (bf16[2,16,4096]{2,1,0:T(8,128)(2,1)S(1)}, bf16[2,16,4096]{2,1,0:T(8,128)(2,1)S(1)}, u32[]{:S(2)}, u32[]{:S(2)}) collective-permute-start(bf16[2,16,4096]{2,1,0:T(8,128)(2,1)S(1)} %pad_maximum_fusion.10), channel_id=1, source_target_pairs={{0,2},{1,3},{2,0},{3,1},{4,6},{5,7},{6,4},{7,5},{8,10},{9,11},{10,... | collective-permute-start | bytes 786440 | tf_op jit(solution)/shard_map/ppermute | solution.py:289
  64.0 8.3 %collective-permute-done.17 = bf16[2,16,4096]{2,1,0:T(8,128)(2,1)S(1)} collective-permute-done((bf16[2,16,4096]{2,1,0:T(8,128)(2,1)S(1)}, bf16[2,16,4096]{2,1,0:T(8,128)(2,1)S(1)}, u32[]{:S(2)}, u32[]{:S(2)}) %collective-permute-start.17) | collective-permute-done | bytes 262176 | tf_op jit(solution)/shard_map/ppermute | solution.py:289
  72.3 3.7 %collective-permute-done.18 = bf16[2,16,4096]{2,1,0:T(8,128)(2,1)S(1)} collective-permute-done((bf16[2,16,4096]{2,1,0:T(8,128)(2,1)S(1)}, bf16[2,16,4096]{2,1,0:T(8,128)(2,1)S(1)}, u32[]{:S(2)}, u32[]{:S(2)}) %collective-permute-start.18) | collective-permute-done | bytes 262176 | tf_op jit(solution)/shard_map/ppermute | solution.py:289
  80.0 2.4 %collective-permute-done.19 = bf16[2,16,4096]{2,1,0:T(8,128)(2,1)S(1)} collective-permute-done((bf16[2,16,4096]{2,1,0:T(8,128)(2,1)S(1)}, bf16[2,16,4096]{2,1,0:T(8,128)(2,1)S(1)}, u32[]{:S(2)}, u32[]{:S(2)}) %collective-permute-start.19) | collective-permute-done | bytes 262176 | tf_op jit(solution)/shard_map/ppermute | solution.py:289
  82.6 5.7 %collective-permute-done.23 = bf16[3,64,1024]{2,1,0:T(8,128)(2,1)S(1)} collective-permute-done((bf16[3,64,1024]{2,1,0:T(8,128)(2,1)S(1)}, bf16[3,64,1024]{2,1,0:T(8,128)(2,1)S(1)}, u32[]{:S(2)}, u32[]{:S(2)}) %collective-permute-start.23) | collective-permute-done | bytes 393248 | tf_op jit(solution)/shard_map/ppermute | solution.py:283
  91.9 5.1 %shard_map.108 = f32[20,128,128]{2,1,0:T(8,128)S(1)} custom-call(s32[1]{0:T(128)} %bitcast.me_ref, s32[20]{0:T(128)S(1)} %copy-done, s32[20]{0:T(128)S(1)} %copy-done.1, s32[20]{0:T(128)S(1)} %copy-done.2, s32[20]{0:T(128)S(1)} %bitcast.196, bf16[2,4,16,4096]{3,2,1,0:T(8,128)(2,1)S(1)} %pad_maximum_fusion.2.refs_0_, ...), custom_call_target="tpu_custom_call" | custom-call | flops 1 | bytes 1 | tf_op jit(solution)/shard_map/pallas_call | solution.py:94
  102.0 15.8 %collective-permute-done.25 = bf16[2,5,64,128]{3,2,1,0:T(8,128)(2,1)S(1)} collective-permute-done((bf16[2,5,64,128]{3,2,1,0:T(8,128)(2,1)S(1)}, bf16[2,5,64,128]{3,2,1,0:T(8,128)(2,1)S(1)}, u32[]{:S(2)}, u32[]{:S(2)}) %collective-permute-start.25) | collective-permute-done | bytes 163872 | tf_op jit(solution)/shard_map/ppermute | solution.py:283
  119.0 3.5 %shard_map.109 = f32[384,1024]{1,0:T(8,128)S(1)} custom-call(bf16[2,2,96,1024]{3,2,1,0:T(8,128)(2,1)S(1)} %maximum_maximum_fusion.refs_0_, bf16[2,2,96,1024]{3,2,1,0:T(8,128)(2,1)S(1)} %collective-permute-done.31.refs_1_, bf16[2,2,96,1024]{3,2,1,0:T(8,128)(2,1)S(1)} %maximum_maximum_fusion.1.refs_2_, ...), custom_call_target="tpu_custom_call" | custom-call | flops 1 | bytes 1 | tf_op jit(solution)/shard_map/pallas_call | solution.py:216
  124.7 1.8 %collective-permute-start.34 = (bf16[4,16,1024]{2,1,0:T(8,128)(2,1)S(1)}, bf16[4,16,1024]{2,1,0:T(8,128)(2,1)S(1)}, u32[]{:S(2)}, u32[]{:S(2)}) collective-permute-start(bf16[4,16,1024]{2,1,0:T(8,128)(2,1)S(1)} %get-tuple-element.202), channel_id=1, source_target_pairs={{0,2},{1,3},{2,0},{3,1},{4,6},{5,7},{6,4},{7,5},{8,10},{9,11},{10,... | collective-permute-start | bytes 393224 | tf_op jit(solution)/shard_map/ppermute | solution.py:289
  126.4 1.6 %collective-permute-start.36 = (bf16[4,16,1024]{2,1,0:T(8,128)(2,1)S(1)}, bf16[4,16,1024]{2,1,0:T(8,128)(2,1)S(1)}, u32[]{:S(2)}, u32[]{:S(2)}) collective-permute-start(bf16[4,16,1024]{2,1,0:T(8,128)(2,1)S(1)} %get-tuple-element.203), channel_id=1, source_target_pairs={{0,4},{1,5},{2,6},{3,7},{4,0},{5,1},{6,2},{7,3},{8,12},{9,13},{10,... | collective-permute-start | bytes 393224 | tf_op jit(solution)/shard_map/ppermute | solution.py:289
  129.1 2.2 %collective-permute-done.34 = bf16[4,16,1024]{2,1,0:T(8,128)(2,1)S(1)} collective-permute-done((bf16[4,16,1024]{2,1,0:T(8,128)(2,1)S(1)}, bf16[4,16,1024]{2,1,0:T(8,128)(2,1)S(1)}, u32[]{:S(2)}, u32[]{:S(2)}) %collective-permute-start.34) | collective-permute-done | bytes 131104 | tf_op jit(solution)/shard_map/ppermute | solution.py:289
  131.6 2.9 %shard_map.110 = f32[128,1024]{1,0:T(8,128)S(1)} custom-call(bf16[2,2,32,1024]{3,2,1,0:T(8,128)(2,1)S(1)} %get-tuple-element.168.refs_0_, bf16[2,2,32,1024]{3,2,1,0:T(8,128)(2,1)S(1)} %collective-permute-done.29.refs_1_, bf16[2,2,32,1024]{3,2,1,0:T(8,128)(2,1)S(1)} %get-tuple-element.169.refs_2_, ...), custom_call_target="tpu_custom_call" | custom-call | flops 1 | bytes 1 | tf_op jit(solution)/shard_map/pallas_call | solution.py:216
  144.3 1.7 %collective-permute-done.40.refs_3_ = bf16[16,1024]{1,0:T(8,128)(2,1)S(1)} collective-permute-done((bf16[16,1024]{1,0:T(8,128)(2,1)S(1)}, bf16[16,1024]{1,0:T(8,128)(2,1)S(1)}, u32[]{:S(2)}, u32[]{:S(2)}) %collective-permute-start.40) | collective-permute-done | bytes 32800 | tf_op jit(solution)/shard_map/ppermute | solution.py:283
  (147 shorter events, 52.1 us)
Async XLA Ops:
  1.6 9.4 %collective-permute-start = (bf16[2,16,1024]{2,1,0:T(8,128)(2,1)S(1)}, bf16[2,16,1024]{2,1,0:T(8,128)(2,1)S(1)}, u32[]{:S(2)}, u32[]{:S(2)}) collective-permute-start(bf16[2,16,1024]{2,1,0:T(8,128)(2,1)S(1)} %pad_maximum_fusion.14), channel_id=1, source_target_pairs={{0,8},{8,0},{16,24},{24,16},{1,9},{9,1},{17,25},{25,17},{2,10},{10... | collective-permute-start | bytes 196616 | tf_op jit(solution)/shard_map/ppermute | solution.py:283
  16.0 12.9 %collective-permute-start.4 = (bf16[3,2,32,1024]{3,2,0,1:T(8,128)(2,1)S(1)}, bf16[3,2,32,1024]{3,2,0,1:T(8,128)(2,1)S(1)}, u32[]{:S(2)}, u32[]{:S(2)}) collective-permute-start(bf16[3,2,32,1024]{3,2,0,1:T(8,128)(2,1)S(1)} %copy.28), channel_id=1, source_target_pairs={{0,8},{8,0},{16,24},{24,16},{1,9},{9,1},{17,25},{25,17},{2,10},{10... | collective-permute-start | bytes 1179656 | tf_op jit(solution)/shard_map/ppermute | solution.py:283
  17.6 11.3 %collective-permute-start.5 = (bf16[3,2,32,1024]{3,2,0,1:T(8,128)(2,1)S(1)}, bf16[3,2,32,1024]{3,2,0,1:T(8,128)(2,1)S(1)}, u32[]{:S(2)}, u32[]{:S(2)}) collective-permute-start(bf16[3,2,32,1024]{3,2,0,1:T(8,128)(2,1)S(1)} %copy.29), channel_id=1, source_target_pairs={{0,16},{8,24},{16,0},{24,8},{1,17},{9,25},{17,1},{25,9},{2,18},{10... | collective-permute-start | bytes 1179656 | tf_op jit(solution)/shard_map/ppermute | solution.py:283
  20.2 15.3 %collective-permute-start.10 = (bf16[2,4,16,1024]{3,2,1,0:T(8,128)(2,1)S(1)}, bf16[2,4,16,1024]{3,2,1,0:T(8,128)(2,1)S(1)}, u32[]{:S(2)}, u32[]{:S(2)}) collective-permute-start(bf16[2,4,16,1024]{3,2,1,0:T(8,128)(2,1)S(1)} %pad_maximum_fusion.7), channel_id=1, source_target_pairs={{0,4},{1,5},{2,6},{3,7},{4,0},{5,1},{6,2},{7,3},{8,12},{9,13},{10,... | collective-permute-start | bytes 786440 | tf_op jit(solution)/shard_map/ppermute | solution.py:289
  25.6 11.3 %collective-permute-start.8 = (bf16[3,2,32,1024]{3,2,0,1:T(8,128)(2,1)S(1)}, bf16[3,2,32,1024]{3,2,0,1:T(8,128)(2,1)S(1)}, u32[]{:S(2)}, u32[]{:S(2)}) collective-permute-start(bf16[3,2,32,1024]{3,2,0,1:T(8,128)(2,1)S(1)} %copy.31), channel_id=1, source_target_pairs={{0,8},{8,0},{16,24},{24,16},{1,9},{9,1},{17,25},{25,17},{2,10},{10... | collective-permute-start | bytes 1179656 | tf_op jit(solution)/shard_map/ppermute | solution.py:283
  27.2 11.0 %collective-permute-start.9 = (bf16[3,2,32,1024]{3,2,0,1:T(8,128)(2,1)S(1)}, bf16[3,2,32,1024]{3,2,0,1:T(8,128)(2,1)S(1)}, u32[]{:S(2)}, u32[]{:S(2)}) collective-permute-start(bf16[3,2,32,1024]{3,2,0,1:T(8,128)(2,1)S(1)} %copy.32), channel_id=1, source_target_pairs={{0,16},{8,24},{16,0},{24,8},{1,17},{9,25},{17,1},{25,9},{2,18},{10... | collective-permute-start | bytes 1179656 | tf_op jit(solution)/shard_map/ppermute | solution.py:283
  38.9 10.2 %collective-permute-start.11 = (bf16[3,64,1024]{2,1,0:T(8,128)(2,1)S(1)}, bf16[3,64,1024]{2,1,0:T(8,128)(2,1)S(1)}, u32[]{:S(2)}, u32[]{:S(2)}) collective-permute-start(bf16[3,64,1024]{2,1,0:T(8,128)(2,1)S(1)} %fusion.2), channel_id=1, source_target_pairs={{0,16},{8,24},{16,0},{24,8},{1,17},{9,25},{17,1},{25,9},{2,18},{10... | collective-permute-start | bytes 1179656 | tf_op jit(solution)/shard_map/ppermute | solution.py:283
  40.5 9.9 %collective-permute-start.12 = (bf16[3,64,1024]{2,1,0:T(8,128)(2,1)S(1)}, bf16[3,64,1024]{2,1,0:T(8,128)(2,1)S(1)}, u32[]{:S(2)}, u32[]{:S(2)}) collective-permute-start(bf16[3,64,1024]{2,1,0:T(8,128)(2,1)S(1)} %fusion.3), channel_id=1, source_target_pairs={{0,8},{8,0},{16,24},{24,16},{1,9},{9,1},{17,25},{25,17},{2,10},{10... | collective-permute-start | bytes 1179656 | tf_op jit(solution)/shard_map/ppermute | solution.py:283
  41.1 10.0 %collective-permute-start.15 = (bf16[2,4,16,1024]{3,2,1,0:T(8,128)(2,1)S(1)}, bf16[2,4,16,1024]{3,2,1,0:T(8,128)(2,1)S(1)}, u32[]{:S(2)}, u32[]{:S(2)}) collective-permute-start(bf16[2,4,16,1024]{3,2,1,0:T(8,128)(2,1)S(1)} %collective-permute-done.10), channel_id=1, source_target_pairs={{0,2},{1,3},{2,0},{3,1},{4,6},{5,7},{6,4},{7,5},{8,10},{9,11},{10,... | collective-permute-start | bytes 786440 | tf_op jit(solution)/shard_map/ppermute | solution.py:289
  51.3 8.7 %collective-permute-start.13 = (bf16[2,64,1024]{2,1,0:T(8,128)(2,1)S(1)}, bf16[2,64,1024]{2,1,0:T(8,128)(2,1)S(1)}, u32[]{:S(2)}, u32[]{:S(2)}) collective-permute-start(bf16[2,64,1024]{2,1,0:T(8,128)(2,1)S(1)} %pad_maximum_fusion.8.refs_6_), channel_id=1, source_target_pairs={{0,16},{8,24},{16,0},{24,8},{1,17},{9,25},{17,1},{25,9},{2,18},{10... | collective-permute-start | bytes 786440 | tf_op jit(solution)/shard_map/ppermute | solution.py:283
  51.9 9.0 %collective-permute-start.14 = (bf16[2,64,1024]{2,1,0:T(8,128)(2,1)S(1)}, bf16[2,64,1024]{2,1,0:T(8,128)(2,1)S(1)}, u32[]{:S(2)}, u32[]{:S(2)}) collective-permute-start(bf16[2,64,1024]{2,1,0:T(8,128)(2,1)S(1)} %pad_maximum_fusion.9.refs_7_), channel_id=1, source_target_pairs={{0,8},{8,0},{16,24},{24,16},{1,9},{9,1},{17,25},{25,17},{2,10},{10... | collective-permute-start | bytes 786440 | tf_op jit(solution)/shard_map/ppermute | solution.py:283
  56.8 20.4 %collective-permute-start.20 = (bf16[3,2,64,1024]{3,2,0,1:T(8,128)(2,1)S(1)}, bf16[3,2,64,1024]{3,2,0,1:T(8,128)(2,1)S(1)}, u32[]{:S(2)}, u32[]{:S(2)}) collective-permute-start(bf16[3,2,64,1024]{3,2,0,1:T(8,128)(2,1)S(1)} %copy.36), channel_id=1, source_target_pairs={{0,8},{8,0},{16,24},{24,16},{1,9},{9,1},{17,25},{25,17},{2,10},{10... | collective-permute-start | bytes 2359304 | tf_op jit(solution)/shard_map/ppermute | solution.py:283
  57.6 19.5 %collective-permute-start.21 = (bf16[3,2,64,1024]{3,2,0,1:T(8,128)(2,1)S(1)}, bf16[3,2,64,1024]{3,2,0,1:T(8,128)(2,1)S(1)}, u32[]{:S(2)}, u32[]{:S(2)}) collective-permute-start(bf16[3,2,64,1024]{3,2,0,1:T(8,128)(2,1)S(1)} %copy.37), channel_id=1, source_target_pairs={{0,16},{8,24},{16,0},{24,8},{1,17},{9,25},{17,1},{25,9},{2,18},{10... | collective-permute-start | bytes 2359304 | tf_op jit(solution)/shard_map/ppermute | solution.py:283
  61.0 11.3 %collective-permute-start.17 = (bf16[2,16,4096]{2,1,0:T(8,128)(2,1)S(1)}, bf16[2,16,4096]{2,1,0:T(8,128)(2,1)S(1)}, u32[]{:S(2)}, u32[]{:S(2)}) collective-permute-start(bf16[2,16,4096]{2,1,0:T(8,128)(2,1)S(1)} %pad_maximum_fusion.10), channel_id=1, source_target_pairs={{0,2},{1,3},{2,0},{3,1},{4,6},{5,7},{6,4},{7,5},{8,10},{9,11},{10,... | collective-permute-start | bytes 786440 | tf_op jit(solution)/shard_map/ppermute | solution.py:289
  62.6 13.4 %collective-permute-start.18 = (bf16[2,16,4096]{2,1,0:T(8,128)(2,1)S(1)}, bf16[2,16,4096]{2,1,0:T(8,128)(2,1)S(1)}, u32[]{:S(2)}, u32[]{:S(2)}) collective-permute-start(bf16[2,16,4096]{2,1,0:T(8,128)(2,1)S(1)} %pad_maximum_fusion.10), channel_id=1, source_target_pairs={{0,4},{1,5},{2,6},{3,7},{4,0},{5,1},{6,2},{7,3},{8,12},{9,13},{10,... | collective-permute-start | bytes 786440 | tf_op jit(solution)/shard_map/ppermute | solution.py:289
  77.8 10.5 %collective-permute-start.23 = (bf16[3,64,1024]{2,1,0:T(8,128)(2,1)S(1)}, bf16[3,64,1024]{2,1,0:T(8,128)(2,1)S(1)}, u32[]{:S(2)}, u32[]{:S(2)}) collective-permute-start(bf16[3,64,1024]{2,1,0:T(8,128)(2,1)S(1)} %fusion.4), channel_id=1, source_target_pairs={{0,16},{8,24},{16,0},{24,8},{1,17},{9,25},{17,1},{25,9},{2,18},{10... | collective-permute-start | bytes 1179656 | tf_op jit(solution)/shard_map/ppermute | solution.py:283
  79.4 10.1 %collective-permute-start.24 = (bf16[3,64,1024]{2,1,0:T(8,128)(2,1)S(1)}, bf16[3,64,1024]{2,1,0:T(8,128)(2,1)S(1)}, u32[]{:S(2)}, u32[]{:S(2)}) collective-permute-start(bf16[3,64,1024]{2,1,0:T(8,128)(2,1)S(1)} %fusion.5), channel_id=1, source_target_pairs={{0,8},{8,0},{16,24},{24,16},{1,9},{9,1},{17,25},{25,17},{2,10},{10... | collective-permute-start | bytes 1179656 | tf_op jit(solution)/shard_map/ppermute | solution.py:283
  82.5 9.3 %collective-permute-start.22 = (bf16[2,4,16,4096]{3,2,1,0:T(8,128)(2,1)S(1)}, bf16[2,4,16,4096]{3,2,1,0:T(8,128)(2,1)S(1)}, u32[]{:S(2)}, u32[]{:S(2)}) collective-permute-start(bf16[2,4,16,4096]{3,2,1,0:T(8,128)(2,1)S(1)} %pad_maximum_fusion.2.refs_0_), channel_id=1, source_target_pairs={{0,1},{1,0},{2,3},{3,2},{4,5},{5,4},{6,7},{7,6},{8,9},{9,8},{10,11... | collective-permute-start | bytes 3145736 | tf_op jit(solution)/shard_map/ppermute | solution.py:286
  97.6 21.4 %collective-permute-start.31 = (bf16[2,2,96,1024]{3,2,1,0:T(8,128)(2,1)S(1)}, bf16[2,2,96,1024]{3,2,1,0:T(8,128)(2,1)S(1)}, u32[]{:S(2)}, u32[]{:S(2)}) collective-permute-start(bf16[2,2,96,1024]{3,2,1,0:T(8,128)(2,1)S(1)} %maximum_maximum_fusion.refs_0_), channel_id=1, source_target_pairs={{0,8},{8,0},{16,24},{24,16},{1,9},{9,1},{17,25},{25,17},{2,10},{10... | collective-permute-start | bytes 2359304 | tf_op jit(solution)/shard_map/ppermute | solution.py:283
  98.6 20.5 %collective-permute-start.32 = (bf16[2,2,96,1024]{3,2,1,0:T(8,128)(2,1)S(1)}, bf16[2,2,96,1024]{3,2,1,0:T(8,128)(2,1)S(1)}, u32[]{:S(2)}, u32[]{:S(2)}) collective-permute-start(bf16[2,2,96,1024]{3,2,1,0:T(8,128)(2,1)S(1)} %maximum_maximum_fusion.1.refs_2_), channel_id=1, source_target_pairs={{0,16},{8,24},{16,0},{24,8},{1,17},{9,25},{17,1},{25,9},{2,18},{10... | collective-permute-start | bytes 2359304 | tf_op jit(solution)/shard_map/ppermute | solution.py:283
  100.1 17.7 %collective-permute-start.25 = (bf16[2,5,64,128]{3,2,1,0:T(8,128)(2,1)S(1)}, bf16[2,5,64,128]{3,2,1,0:T(8,128)(2,1)S(1)}, u32[]{:S(2)}, u32[]{:S(2)}) collective-permute-start(bf16[2,5,64,128]{3,2,1,0:T(8,128)(2,1)S(1)} %fusion.30), channel_id=1, source_target_pairs={{0,8},{8,0},{16,24},{24,16},{1,9},{9,1},{17,25},{25,17},{2,10},{10... | collective-permute-start | bytes 491528 | tf_op jit(solution)/shard_map/ppermute | solution.py:283
  101.4 17.5 %collective-permute-start.26 = (bf16[2,5,64,128]{3,2,1,0:T(8,128)(2,1)S(1)}, bf16[2,5,64,128]{3,2,1,0:T(8,128)(2,1)S(1)}, u32[]{:S(2)}, u32[]{:S(2)}) collective-permute-start(bf16[2,5,64,128]{3,2,1,0:T(8,128)(2,1)S(1)} %fusion.31), channel_id=1, source_target_pairs={{0,16},{8,24},{16,0},{24,8},{1,17},{9,25},{17,1},{25,9},{2,18},{10... | collective-permute-start | bytes 491528 | tf_op jit(solution)/shard_map/ppermute | solution.py:283
  126.4 12.6 %collective-permute-start.36 = (bf16[4,16,1024]{2,1,0:T(8,128)(2,1)S(1)}, bf16[4,16,1024]{2,1,0:T(8,128)(2,1)S(1)}, u32[]{:S(2)}, u32[]{:S(2)}) collective-permute-start(bf16[4,16,1024]{2,1,0:T(8,128)(2,1)S(1)} %get-tuple-element.203), channel_id=1, source_target_pairs={{0,4},{1,5},{2,6},{3,7},{4,0},{5,1},{6,2},{7,3},{8,12},{9,13},{10,... | collective-permute-start | bytes 393224 | tf_op jit(solution)/shard_map/ppermute | solution.py:289
  128.0 11.0 %collective-permute-start.37 = (bf16[4,16,1024]{2,1,0:T(8,128)(2,1)S(1)}, bf16[4,16,1024]{2,1,0:T(8,128)(2,1)S(1)}, u32[]{:S(2)}, u32[]{:S(2)}) collective-permute-start(bf16[4,16,1024]{2,1,0:T(8,128)(2,1)S(1)} %get-tuple-element.204), channel_id=1, source_target_pairs={{0,6},{1,7},{2,4},{3,5},{4,2},{5,3},{6,0},{7,1},{8,14},{9,15},{10,... | collective-permute-start | bytes 393224 | tf_op jit(solution)/shard_map/ppermute | solution.py:289
  (25 other events, 118.3 us)
